TPU v7x, 256 devices: a whole 4x4x8 slice. The times are simulated.
256 devices in a mesh: trans: 64 (over x, y, z_hi, core), pw: 4 (over z_lo).
Axes of the slice: x: 4, y: 4, z: 8 (z_hi: 2, z_lo: 4; z = z_hi * 4 + z_lo), core: 2. Of those that a mesh axis runs over, the one named last changes fastest.
Arguments:
- pair_density: bfloat16 [32768, 8192], P('trans', 'pw'), may hold values from -0.3984375 to 0.3984375
- coulomb: float32 [8192], P('pw'), may hold values from 0.1 to 10
- partners: int32 [64, 4], P('trans'), may hold values from 0 to 63, as said below
Outputs:
- kernel_tiles: float32 [256, 512, 512], P('trans', None, 'pw')
Inputs may be any that keep to these rules, and one draw needn't show every extreme that they name: partners[i, s] = (i + o) mod 64 for an offset o of 1 to 6; the offsets of one row are distinct.
All inputs are finite; a program needn't handle non-finite values.
Results may differ from a plain program's by a relative error of at most 0.014.
Values may be sent and summed in bfloat16 or wider, within the bound.
No kernel may reach another device: no remote copies, remote signals or barrier semaphores. Data moves between devices by JAX's collectives and lax.ppermute only.
A program may use at most 128 MiB of HBM per device.

v0:
```python
import jax
import jax.numpy as jnp
from jax import lax
from jax.sharding import PartitionSpec as P

SLOTS = 4


def shifted(value, axis, steps):
    count = lax.axis_size(axis)
    pairs = [(source, (source + steps) % count) for source in range(count)]
    return lax.ppermute(value, axis, pairs)


def band_blocks(moving, span):
    blocks = []
    current = moving
    for step in range(1, span + 1):
        current = shifted(current, "trans", -1)
        blocks.append(current)
    return jnp.stack(blocks)


def body(pair_density, coulomb, partners):
    count = lax.axis_size("trans")
    mine = lax.axis_index("trans")
    span = SLOTS + 2
    offsets = (partners[0] - mine) % count - 1
    weighted = (pair_density.astype(jnp.float32) * coulomb[None, :]).astype(jnp.bfloat16)
    stacked = band_blocks(pair_density, span)
    tiles = []
    for slot in range(SLOTS):
        partner = lax.dynamic_index_in_dim(stacked, offsets[slot], 0, keepdims=False)
        tiles.append(
            lax.dot_general(
                weighted, partner, (((1,), (1,)), ((), ())), preferred_element_type=jnp.float32
            )
        )
    tiles = jnp.stack(tiles)
    return lax.psum_scatter(tiles, "pw", scatter_dimension=2, tiled=True)


def solution(mesh):
    placed = (P("trans", "pw"), P("pw"), P("trans", None))
    return jax.shard_map(
        body, mesh=mesh, in_specs=placed, out_specs=P("trans", None, "pw"), check_vma=False
    )
```

profile of v0, /device:TPU:6, one launch (start us, length us, event | category | flops | bytes accessed | tf_op | source)
XLA Modules:
  0.0 440.5 jit_solution(17235184478977662321)
XLA Ops:
  6.5 0.0 reduce-scatter.2.cloned.1.call-start
  6.5 9.3 %collective-permute-start = (bf16[512,2048]{1,0:T(8,128)(2,1)}, bf16[512,2048]{1,0:T(8,128)(2,1)S(1)}, u32[]{:S(2)}, u32[]{:S(2)}) collective-permute-start(bf16[512,2048]{1,0:T(8,128)(2,1)} %param.3), channel_id=1, source_target_pairs={{0,252},{4,0},{8,4},{12,8},{16,12},{20,16},{24,20},{28,24},{32,28}... | collective-permute-start | bytes 6291464 | tf_op jit(solution)/shard_map/ppermute | solution.py:12
  15.9 45.5 %collective-permute-done = bf16[512,2048]{1,0:T(8,128)(2,1)S(1)} collective-permute-done((bf16[512,2048]{1,0:T(8,128)(2,1)}, bf16[512,2048]{1,0:T(8,128)(2,1)S(1)}, u32[]{:S(2)}, u32[]{:S(2)}) %collective-permute-start) | collective-permute-done | bytes 2097184 | tf_op jit(solution)/shard_map/ppermute | solution.py:12
  61.4 0.0 copy-start
  61.4 8.8 %collective-permute-start.1 = (bf16[512,2048]{1,0:T(8,128)(2,1)S(1)}, bf16[512,2048]{1,0:T(8,128)(2,1)S(1)}, u32[]{:S(2)}, u32[]{:S(2)}) collective-permute-start(bf16[512,2048]{1,0:T(8,128)(2,1)S(1)} %collective-permute-done), channel_id=1, source_target_pairs={{0,252},{4,0},{8,4},{12,8},{16,12},{20,16},{24,20},{28,24},{32,28}... | collective-permute-start | bytes 6291464 | tf_op jit(solution)/shard_map/ppermute | solution.py:12
  70.2 46.5 %collective-permute-done.1 = bf16[512,2048]{1,0:T(8,128)(2,1)S(1)} collective-permute-done((bf16[512,2048]{1,0:T(8,128)(2,1)S(1)}, bf16[512,2048]{1,0:T(8,128)(2,1)S(1)}, u32[]{:S(2)}, u32[]{:S(2)}) %collective-permute-start.1) | collective-permute-done | bytes 2097184 | tf_op jit(solution)/shard_map/ppermute | solution.py:12
  116.6 8.9 %collective-permute-start.2 = (bf16[512,2048]{1,0:T(8,128)(2,1)S(1)}, bf16[512,2048]{1,0:T(8,128)(2,1)S(1)}, u32[]{:S(2)}, u32[]{:S(2)}) collective-permute-start(bf16[512,2048]{1,0:T(8,128)(2,1)S(1)} %collective-permute-done.1), channel_id=1, source_target_pairs={{0,252},{4,0},{8,4},{12,8},{16,12},{20,16},{24,20},{28,24},{32,28}... | collective-permute-start | bytes 6291464 | tf_op jit(solution)/shard_map/ppermute | solution.py:12
  125.5 63.5 %collective-permute-done.2 = bf16[512,2048]{1,0:T(8,128)(2,1)S(1)} collective-permute-done((bf16[512,2048]{1,0:T(8,128)(2,1)S(1)}, bf16[512,2048]{1,0:T(8,128)(2,1)S(1)}, u32[]{:S(2)}, u32[]{:S(2)}) %collective-permute-start.2) | collective-permute-done | bytes 2097184 | tf_op jit(solution)/shard_map/ppermute | solution.py:12
  189.0 0.0 copy-done
  189.0 0.0 copy-start.1
  189.0 8.9 %collective-permute-start.3 = (bf16[512,2048]{1,0:T(8,128)(2,1)S(1)}, bf16[512,2048]{1,0:T(8,128)(2,1)}, u32[]{:S(2)}, u32[]{:S(2)}) collective-permute-start(bf16[512,2048]{1,0:T(8,128)(2,1)S(1)} %collective-permute-done.2), channel_id=1, source_target_pairs={{0,252},{4,0},{8,4},{12,8},{16,12},{20,16},{24,20},{28,24},{32,28}... | collective-permute-start | bytes 6291464 | tf_op jit(solution)/shard_map/ppermute | solution.py:12
  197.9 0.0 copy-done.1
  197.9 63.7 %collective-permute-done.3 = bf16[512,2048]{1,0:T(8,128)(2,1)} collective-permute-done((bf16[512,2048]{1,0:T(8,128)(2,1)S(1)}, bf16[512,2048]{1,0:T(8,128)(2,1)}, u32[]{:S(2)}, u32[]{:S(2)}) %collective-permute-start.3) | collective-permute-done | bytes 2097184 | tf_op jit(solution)/shard_map/ppermute | solution.py:12
  261.6 9.0 %collective-permute-start.4 = (bf16[512,2048]{1,0:T(8,128)(2,1)}, bf16[512,2048]{1,0:T(8,128)(2,1)}, u32[]{:S(2)}, u32[]{:S(2)}) collective-permute-start(bf16[512,2048]{1,0:T(8,128)(2,1)} %collective-permute-done.3), channel_id=1, source_target_pairs={{0,252},{4,0},{8,4},{12,8},{16,12},{20,16},{24,20},{28,24},{32,28}... | collective-permute-start | bytes 6291464 | tf_op jit(solution)/shard_map/ppermute | solution.py:12
  270.6 0.7 fusion.28
  271.3 0.7 fusion.30
  279.5 0.0 copy-start.2
  279.5 1.9 bitcast_dynamic-update-slice_fusion.5
  281.4 13.1 %collective-permute-done.4 = bf16[512,2048]{1,0:T(8,128)(2,1)} collective-permute-done((bf16[512,2048]{1,0:T(8,128)(2,1)}, bf16[512,2048]{1,0:T(8,128)(2,1)}, u32[]{:S(2)}, u32[]{:S(2)}) %collective-permute-start.4) | collective-permute-done | bytes 2097184 | tf_op jit(solution)/shard_map/ppermute | solution.py:12
  294.5 8.8 %collective-permute-start.5 = (bf16[512,2048]{1,0:T(8,128)(2,1)}, bf16[512,2048]{1,0:T(8,128)(2,1)S(1)}, u32[]{:S(2)}, u32[]{:S(2)}) collective-permute-start(bf16[512,2048]{1,0:T(8,128)(2,1)} %collective-permute-done.4), channel_id=1, source_target_pairs={{0,252},{4,0},{8,4},{12,8},{16,12},{20,16},{24,20},{28,24},{32,28}... | collective-permute-start | bytes 6291464 | tf_op jit(solution)/shard_map/ppermute | solution.py:12
  303.3 0.1 bitcast_dynamic-update-slice_fusion.4
  303.4 0.0 copy-done.2
  303.4 0.1 bitcast_dynamic-update-slice_fusion.3
  303.6 1.7 bitcast_dynamic-update-slice_fusion.2
  305.3 0.0 copy-start.3
  305.3 0.0 copy-start.4
  305.4 1.9 bitcast_dynamic-update-slice_fusion.1
  307.2 19.9 %collective-permute-done.5 = bf16[512,2048]{1,0:T(8,128)(2,1)S(1)} collective-permute-done((bf16[512,2048]{1,0:T(8,128)(2,1)}, bf16[512,2048]{1,0:T(8,128)(2,1)S(1)}, u32[]{:S(2)}, u32[]{:S(2)}) %collective-permute-start.5) | collective-permute-done | bytes 2097184 | tf_op jit(solution)/shard_map/ppermute | solution.py:12
  327.2 0.1 bitcast_dynamic-update-slice_fusion
  327.3 0.0 copy-done.3
  327.3 0.0 copy-done.4
  327.3 1.3 fusion.12
  328.6 1.3 fusion.15
  329.9 1.3 fusion.18
  331.2 1.3 fusion.21
  332.5 2.4 pad_maximum_fusion
  334.9 0.0 reduce-scatter.2.cloned.1.call-update
  335.0 98.7 %reduce-scatter.2.cloned.1.call-done = f32[4,512,128]{2,1,0:T(8,128)} async-done(((f32[4,512,512]{2,1,0:T(8,128)}), f32[4,512,128]{2,1,0:T(8,128)}) %reduce-scatter.2.cloned.1.call-update) | async-done | bytes 1048592 | tf_op jit(solution)/shard_map/reduce_scatter | solution.py:40
Async XLA Ops:
  6.5 427.1 %reduce-scatter.2.cloned.1.call-start = ((), (), s32[]{:S(2)}) async-start(), calls=%async_computation.1 | async-start | bytes 5242880 | tf_op jit(solution)/shard_map/reduce_scatter | solution.py:40
  6.5 54.9 %collective-permute-start = (bf16[512,2048]{1,0:T(8,128)(2,1)}, bf16[512,2048]{1,0:T(8,128)(2,1)S(1)}, u32[]{:S(2)}, u32[]{:S(2)}) collective-permute-start(bf16[512,2048]{1,0:T(8,128)(2,1)} %param.3), channel_id=1, source_target_pairs={{0,252},{4,0},{8,4},{12,8},{16,12},{20,16},{24,20},{28,24},{32,28}... | collective-permute-start | bytes 6291464 | tf_op jit(solution)/shard_map/ppermute | solution.py:12
  61.4 127.6 %copy-start = (bf16[512,2048]{1,0:T(8,128)(2,1)}, bf16[512,2048]{1,0:T(8,128)(2,1)S(1)}, u32[]{:S(2)}) copy-start(bf16[512,2048]{1,0:T(8,128)(2,1)S(1)} %collective-permute-done) | copy-start | bytes 6291460
  61.4 55.2 %collective-permute-start.1 = (bf16[512,2048]{1,0:T(8,128)(2,1)S(1)}, bf16[512,2048]{1,0:T(8,128)(2,1)S(1)}, u32[]{:S(2)}, u32[]{:S(2)}) collective-permute-start(bf16[512,2048]{1,0:T(8,128)(2,1)S(1)} %collective-permute-done), channel_id=1, source_target_pairs={{0,252},{4,0},{8,4},{12,8},{16,12},{20,16},{24,20},{28,24},{32,28}... | collective-permute-start | bytes 6291464 | tf_op jit(solution)/shard_map/ppermute | solution.py:12
  116.6 72.4 %collective-permute-start.2 = (bf16[512,2048]{1,0:T(8,128)(2,1)S(1)}, bf16[512,2048]{1,0:T(8,128)(2,1)S(1)}, u32[]{:S(2)}, u32[]{:S(2)}) collective-permute-start(bf16[512,2048]{1,0:T(8,128)(2,1)S(1)} %collective-permute-done.1), channel_id=1, source_target_pairs={{0,252},{4,0},{8,4},{12,8},{16,12},{20,16},{24,20},{28,24},{32,28}... | collective-permute-start | bytes 6291464 | tf_op jit(solution)/shard_map/ppermute | solution.py:12
  189.0 8.9 %copy-start.1 = (bf16[512,2048]{1,0:T(8,128)(2,1)}, bf16[512,2048]{1,0:T(8,128)(2,1)S(1)}, u32[]{:S(2)}) copy-start(bf16[512,2048]{1,0:T(8,128)(2,1)S(1)} %collective-permute-done.2) | copy-start | bytes 6291460
  189.0 72.6 %collective-permute-start.3 = (bf16[512,2048]{1,0:T(8,128)(2,1)S(1)}, bf16[512,2048]{1,0:T(8,128)(2,1)}, u32[]{:S(2)}, u32[]{:S(2)}) collective-permute-start(bf16[512,2048]{1,0:T(8,128)(2,1)S(1)} %collective-permute-done.2), channel_id=1, source_target_pairs={{0,252},{4,0},{8,4},{12,8},{16,12},{20,16},{24,20},{28,24},{32,28}... | collective-permute-start | bytes 6291464 | tf_op jit(solution)/shard_map/ppermute | solution.py:12
  261.6 32.8 %collective-permute-start.4 = (bf16[512,2048]{1,0:T(8,128)(2,1)}, bf16[512,2048]{1,0:T(8,128)(2,1)}, u32[]{:S(2)}, u32[]{:S(2)}) collective-permute-start(bf16[512,2048]{1,0:T(8,128)(2,1)} %collective-permute-done.3), channel_id=1, source_target_pairs={{0,252},{4,0},{8,4},{12,8},{16,12},{20,16},{24,20},{28,24},{32,28}... | collective-permute-start | bytes 6291464 | tf_op jit(solution)/shard_map/ppermute | solution.py:12
  279.5 24.0 %copy-start.2 = (bf16[512,2048]{1,0:T(8,128)(2,1)S(1)}, bf16[512,2048]{1,0:T(8,128)(2,1)}, u32[]{:S(2)}) copy-start(bf16[512,2048]{1,0:T(8,128)(2,1)} %copy-done.1) | copy-start | bytes 6291460
  294.5 32.7 %collective-permute-start.5 = (bf16[512,2048]{1,0:T(8,128)(2,1)}, bf16[512,2048]{1,0:T(8,128)(2,1)S(1)}, u32[]{:S(2)}, u32[]{:S(2)}) collective-permute-start(bf16[512,2048]{1,0:T(8,128)(2,1)} %collective-permute-done.4), channel_id=1, source_target_pairs={{0,252},{4,0},{8,4},{12,8},{16,12},{20,16},{24,20},{28,24},{32,28}... | collective-permute-start | bytes 6291464 | tf_op jit(solution)/shard_map/ppermute | solution.py:12
  305.3 22.0 %copy-start.3 = (bf16[512,2048]{1,0:T(8,128)(2,1)S(1)}, bf16[512,2048]{1,0:T(8,128)(2,1)}, u32[]{:S(2)}) copy-start(bf16[512,2048]{1,0:T(8,128)(2,1)} %param.3) | copy-start | bytes 6291460
  305.3 22.0 %copy-start.4 = (f32[2048]{0:T(1024)S(1)}, f32[2048]{0:T(1024)}, u32[]{:S(2)}) copy-start(f32[2048]{0:T(1024)} %param.4) | copy-start | bytes 24580
Sparse Core Ops, SparseCore 0:
  335.1 98.5 reduce-scatter.1
where the time goes:
time: 441 us; the launch traced here: 440 us
  waiting for transfers between devices  351 us (80%)
  starting transfers between devices  53.7 us (12%)
  between operations  21 us (5%)
  local copies, waits for them, and re-layouts  6.58 us (1%)
  matrix products  5.19 us (1%)
    ppermute x6, waiting for transfers between devices, shifted(): return lax.ppermute(value, axis, pairs)  252 us
    reduce_scatter x1, waiting for transfers between devices, body(): return lax.psum_scatter(tiles, 'pw', scatter_dimension=2, tiled=True)  98.7 us
    ppermute x6, starting transfers between devices, shifted(): return lax.ppermute(value, axis, pairs)  53.7 us
  transfers between devices with their start and end apart: 7, of which 7 were waited for; matrix products, arithmetic and copies ran while one was open for 2% of the time, Pallas kernels for 0%

commit v1 on v0

v1 whole, which is shorter than its diff:
```python
import functools

import jax
import jax.numpy as jnp
from jax import lax
from jax.experimental import pallas as pl
from jax.experimental.pallas import tpu as pltpu
from jax.sharding import PartitionSpec as P

SLOTS = 4
TB = 512
PIECES = 2
AXES = ("trans", "pw")


def place(device):
    trans, pw = divmod(device, 4)
    return trans // 16, trans // 4 % 4, trans // 2 % 2 * 4 + pw, trans % 2


def device_at(x, y, z, core):
    z %= 8
    return (((x % 4 * 4 + y % 4) * 2 + z // 4) * 2 + core) * 4 + z % 4


def send(value, target):
    pairs = []
    for device in range(256):
        there = target(*place(device))
        if there is not None:
            pairs.append((device, device_at(*there)))
    return lax.ppermute(value, AXES, pairs)


def other_half(x, y, z, core):
    return x, y, z + 4, core


def other_core(x, y, z, core):
    return x, y, z, 1 - core


def previous_column(x, y, z, core):
    column = (x * 4 + y - 1) % 16
    return column // 4, column % 4, z, core


def up_one(x, y, z, core):
    return x, y + 1, z, core


def up_to_owner(from_core, x, y, z, core):
    if core != from_core:
        return None
    return (x if y in (3, 0) else x - 1), y + 1, z, 1


def tile_kernel(pieces, table, coulomb, *refs):
    blocks, (out, weighted, held, sems) = refs[:-4], refs[-4:]
    groups = []
    at = 0
    for count in (1, 1, pieces, pieces, 1, 1, pieces, pieces, pieces, pieces):
        groups.append(blocks[at : at + count])
        at += count

    def fetch(number, slot, choices):
        for index in choices:

            @pl.when(number == index)
            def _():
                group = groups[index]
                width = 1024 // len(group)
                for part, ref in enumerate(group):
                    pltpu.make_async_copy(
                        ref, held.at[slot, :, pl.ds(part * width, width)], sems.at[slot]
                    ).start()

    def arrived(slot):
        pltpu.make_async_copy(held.at[slot], held.at[slot], sems.at[slot]).wait()

    fetch(table[0], 0, range(4))
    fetch(table[1], 1, range(4))
    for owner in range(2):
        arrived(owner)
        weighted[owner] = (held[owner].astype(jnp.float32) * coulomb[...]).astype(jnp.bfloat16)
        fetch(table[2 + owner], owner, range(10))

    def step(tile, carry):
        slot = tile % 2
        arrived(slot)
        result = lax.dot_general(
            weighted[tile // SLOTS], held[slot], (((1,), (1,)), ((), ())), preferred_element_type=jnp.float32
        ).astype(jnp.bfloat16)
        for part in range(4):
            out[part, tile] = result[:, part * 128 : (part + 1) * 128]

        @pl.when(tile < 2 * SLOTS - 2)
        def _():
            fetch(table[4 + tile], slot, range(10))

        return carry

    lax.fori_loop(0, 2 * SLOTS, step, 0)


def partial_tiles(table, coulomb, blocks):
    any_spec = pl.BlockSpec(memory_space=pl.ANY)
    return pl.pallas_call(
        functools.partial(tile_kernel, PIECES),
        out_shape=jax.ShapeDtypeStruct((4, 2 * SLOTS, TB, 128), jnp.bfloat16),
        in_specs=[
            pl.BlockSpec(memory_space=pltpu.SMEM),
            pl.BlockSpec(memory_space=pltpu.VMEM),
        ]
        + [any_spec] * len(blocks),
        out_specs=pl.BlockSpec(memory_space=pltpu.VMEM),
        scratch_shapes=[
            pltpu.VMEM((2, TB, 1024), jnp.bfloat16),
            pltpu.VMEM((2, TB, 1024), jnp.bfloat16),
            pltpu.SemaphoreType.DMA((2,)),
        ],
        compiler_params=pltpu.CompilerParams(vmem_limit_bytes=32 * 1024 * 1024),
        cost_estimate=pl.CostEstimate(flops=8 * 2 * TB * TB * 1024, bytes_accessed=12 << 20, transcendentals=0),
    )(table, coulomb, *blocks)


def chain(tiles, owner, way, pw):
    arriving = None
    far = 4 if (way < 0) == (owner == 0) else 3
    for distance in range(far, 0, -1):
        part = lax.dynamic_index_in_dim(tiles, (pw + way * distance) % 4, 0, keepdims=False)
        part = part[owner * SLOTS : (owner + 1) * SLOTS]
        if arriving is not None:
            part = (part.astype(jnp.float32) + arriving.astype(jnp.float32)).astype(jnp.bfloat16)

        def target(x, y, z, core, distance=distance):
            half = (z + way * distance) % 8 // 4
            if core != half:
                return None
            return x, y, z + way, (half if distance > 1 else owner)

        arriving = send(part, target)
    return arriving


def body(pair_density, coulomb, partners):
    mine = lax.axis_index("trans")
    pw = lax.axis_index("pw")
    core = mine % 2
    half = mine // 2 % 2
    width = 1024 // PIECES
    away = [
        lax.dynamic_slice_in_dim(pair_density, (1 - half) * 1024 + i * width, width, 1) for i in range(PIECES)
    ]
    other = [send(piece, other_half) for piece in away]
    keep = lax.dynamic_slice_in_dim(pair_density, half * 1024, 1024, 1)
    keep_next = send(keep, previous_column)
    offsets = (partners - mine) % 64
    both = send(offsets, other_core)
    both = jnp.where(core == 0, jnp.concatenate([offsets, both]), jnp.concatenate([both, offsets]))
    far = send(both, other_half)
    wanted = jnp.where(half == core, both, far)
    keep_swap = send(keep, other_core)
    keep_next_swap = send(keep_next, other_core)
    other_swap, other_next, other_next_swap, last_0, last_1 = [], [], [], [], []
    for i, piece in enumerate(other):
        first = jnp.where(half == 0, keep[:, i * width : (i + 1) * width], piece)
        moved = send(first, up_one)
        follow = send(piece, previous_column)
        other_next.append(follow)
        last_0.append(send(moved, functools.partial(up_to_owner, 0)))
        last_1.append(send(moved, functools.partial(up_to_owner, 1)))
        other_swap.append(send(piece, other_core))
        other_next_swap.append(send(follow, other_core))
    owners = jnp.arange(2, dtype=jnp.int32)
    own_entry = 2 * (core ^ half) + (owners ^ core)
    number = owners[:, None] + wanted + 2 * core
    pair = number // 2
    low = number % 2
    entry = jnp.where(pair < 4, 2 * (pair ^ half) + (low ^ core), 8 + low)
    table = jnp.concatenate([own_entry, entry.reshape(-1)]).astype(jnp.int32)
    weights = lax.dynamic_slice_in_dim(coulomb, half * 1024, 1024, 0).reshape(1, 1024)
    blocks = [keep, keep_swap, *other, *other_swap, keep_next, keep_next_swap, *other_next, *other_next_swap]
    tiles = partial_tiles(table, weights, blocks + last_0 + last_1)
    down_0, up_1 = chain(tiles, 0, -1, pw), chain(tiles, 1, 1, pw)
    down_1, up_0 = chain(tiles, 1, -1, pw), chain(tiles, 0, 1, pw)
    here = lax.dynamic_index_in_dim(tiles, pw, 0, keepdims=False)
    given = send(
        lax.dynamic_slice_in_dim(here, (1 - half) * SLOTS, SLOTS, 0),
        lambda x, y, z, c: (x, y, z, 1 - c) if c == z // 4 else None,
    )
    held = lax.dynamic_slice_in_dim(here, half * SLOTS, SLOTS, 0)
    total = jnp.where(core == half, held, given).astype(jnp.float32)
    total += jnp.where(core == 0, down_0, down_1).astype(jnp.float32)
    return total + jnp.where(core == 0, up_0, up_1).astype(jnp.float32)


def solution(mesh):
    placed = (P("trans", "pw"), P("pw"), P("trans", None))
    return jax.shard_map(
        body, mesh=mesh, in_specs=placed, out_specs=P("trans", None, "pw"), check_vma=False
    )
```

time: 441 us -> 218 us (0.49)
  waiting for transfers between devices: 351 us -> 99.9 us
  starting transfers between devices: 53.7 us -> 77.3 us
  between operations: 21 us -> 0.31 us
  other arithmetic: 3.06 us -> 13.7 us
  Pallas kernels: 0 us -> 9.76 us
  local copies, waits for them, and re-layouts: 6.58 us -> 14.2 us
  matrix products: 5.19 us -> 0 us
    ppermute x6 -> x34, waiting for transfers between devices: 252 us -> 99.9 us  [send(): return lax.ppermute(value, AXES, pairs)]
    reduce_scatter x1 -> x0, waiting for transfers between devices: 98.7 us -> none  [body(): return lax.psum_scatter(tiles, 'pw', scatter_dimension=2, tiled=True)]
    ppermute x6 -> x34, starting transfers between devices: 53.7 us -> 77.3 us  [send(): return lax.ppermute(value, AXES, pairs)]
    pallas_call x0 -> x1, Pallas kernels: none -> 9.76 us  [partial_tiles(): pl.pallas_call(functools.partial(tile_kernel, PIECES), out_shape=jax.Shap...]
    convert_element_type x0 -> x5, other arithmetic: none -> 8.36 us  [chain(): (part.astype(jnp.float32) + arriving.astype(jnp.float32)).astype(jnp.bflo...]
    dot_general x4 -> x0, matrix products: 5.19 us -> none  [body(): lax.dot_general(weighted, partner, (((1,), (1,)), ((), ())), preferred_el...]
    unnamed x15 -> x22, local copies, waits for them, and re-layouts: 5.78 us -> 9.33 us
  transfers between devices with their start and end apart: 7 -> 34, of which waited for: 7 -> 14; matrix products, arithmetic and copies ran while one was open for 2% -> 4% of each run, Pallas kernels for 0% -> 0%
where the time goes in v1:
time: 218 us; the launch traced here: 215 us
  waiting for transfers between devices  99.9 us (46%)
  starting transfers between devices  77.3 us (35%)
  local copies, waits for them, and re-layouts  14.2 us (7%)
  other arithmetic  13.7 us (6%)
  Pallas kernels  9.76 us (4%)
    ppermute x34, waiting for transfers between devices, send(): return lax.ppermute(value, AXES, pairs)  99.9 us
    ppermute x34, starting transfers between devices, send(): return lax.ppermute(value, AXES, pairs)  77.3 us
    pallas_call x1, Pallas kernels, partial_tiles(): pl.pallas_call(functools.partial(tile_kernel, PIECES), out_shape=jax.Shap...  9.76 us
    unnamed x22, local copies, waits for them, and re-layouts  9.33 us
    convert_element_type x5, other arithmetic, chain(): (part.astype(jnp.float32) + arriving.astype(jnp.float32)).astype(jnp.bflo...  8.36 us
  transfers between devices with their start and end apart: 34, of which 14 were waited for; matrix products, arithmetic and copies ran while one was open for 4% of the time, Pallas kernels for 0%

profile of v1, /device:TPU:6, one launch (start us, length us, event | category | flops | bytes accessed | tf_op | source)
XLA Modules:
  0.0 215.1 jit_solution(16509456332889268428)
XLA Ops:
  0.0 2.3 %constant_dynamic-slice_fusion = (bf16[512,512]{1,0:T(8,128)(2,1)}, bf16[512,512]{1,0:T(8,128)(2,1)}) fusion(bf16[512,2048]{1,0:T(8,128)(2,1)} %param.3, s32[]{:T(128)S(6)} %select_n.193, s32[]{:T(128)S(6)} %select_n.192), kind=kLoop, calls=%fused_computation.39 | loop fusion | bytes 2097160 | tf_op jit(solution)/shard_map/dynamic_slice | solution.py:153
  2.3 7.2 %collective-permute-start.3 = (bf16[512,512]{1,0:T(8,128)(2,1)}, bf16[512,512]{1,0:T(8,128)(2,1)S(1)}, u32[]{:S(2)}, u32[]{:S(2)}) collective-permute-start(bf16[512,512]{1,0:T(8,128)(2,1)} %get-tuple-element.20), channel_id=1, source_target_pairs={{0,8},{1,9},{2,10},{3,11},{4,12},{5,13},{6,14},{7,15},{8,0},{9,1},... | collective-permute-start | bytes 1572872 | tf_op jit(solution)/shard_map/ppermute | solution.py:32
  9.5 1.3 constant_dynamic-slice_fusion.2.refs_0_
  10.8 3.4 %collective-permute-start.7 = (bf16[512,1024]{1,0:T(8,128)(2,1)S(1)}, bf16[512,1024]{1,0:T(8,128)(2,1)S(1)}, u32[]{:S(2)}, u32[]{:S(2)}) collective-permute-start(bf16[512,1024]{1,0:T(8,128)(2,1)S(1)} %constant_dynamic-slice_fusion.2.refs_0_), channel_id=1, source_target_pairs={{0,240},{1,241},{2,242},{3,243},{4,244},{5,245},{6,246},{7,247},{8... | collective-permute-start | bytes 3145736 | tf_op jit(solution)/shard_map/ppermute | solution.py:32
  14.2 10.5 %collective-permute-done.3.refs_2_ = bf16[512,512]{1,0:T(8,128)(2,1)S(1)} collective-permute-done((bf16[512,512]{1,0:T(8,128)(2,1)}, bf16[512,512]{1,0:T(8,128)(2,1)S(1)}, u32[]{:S(2)}, u32[]{:S(2)}) %collective-permute-start.3) | collective-permute-done | bytes 524320 | tf_op jit(solution)/shard_map/ppermute | solution.py:32
  24.7 29.5 %collective-permute-done.4.refs_3_ = bf16[512,512]{1,0:T(8,128)(2,1)S(1)} collective-permute-done((bf16[512,512]{1,0:T(8,128)(2,1)}, bf16[512,512]{1,0:T(8,128)(2,1)S(1)}, u32[]{:S(2)}, u32[]{:S(2)}) %collective-permute-start.4) | collective-permute-done | bytes 524320 | tf_op jit(solution)/shard_map/ppermute | solution.py:32
  54.2 2.5 %dynamic-slice_select_fusion = (bf16[512,512]{1,0:T(8,128)(2,1)}, bf16[512,512]{1,0:T(8,128)(2,1)}) fusion(bf16[512,512]{1,0:T(8,128)(2,1)S(1)} %collective-permute-done.4.refs_3_, bf16[512,2048]{1,0:T(8,128)(2,1)} %param.3, s32[]{:T(128)S(6)} %add.261, pred[]{:T(512)S(6)} %eq.39, bf16[512,512]{1,0:T(8,128)(2,1)S(1)} %collective-permute-done.3.refs_2_, ...), kind=kLoop, calls=%fused_computation.35 | loop fusion | flops 524288 | bytes 3145737 | tf_op jit(solution)/shard_map/jit(_where)/select_n | solution.py:167
  56.7 1.6 collective-permute-start.13
  58.2 1.6 collective-permute-start.15
  59.8 0.6 collective-permute-start
  60.4 1.7 collective-permute-done
  62.1 6.4 %collective-permute-start.1 = (s32[2,4]{1,0:T(2,128)S(1)}, s32[2,4]{1,0:T(2,128)S(1)}, u32[]{:S(2)}, u32[]{:S(2)}) collective-permute-start(s32[2,4]{1,0:T(2,128)S(1)} %add_select_fusion), channel_id=1, source_target_pairs={{0,8},{1,9},{2,10},{3,11},{4,12},{5,13},{6,14},{7,15},{8,0},{9,1},... | collective-permute-start | bytes 104 | tf_op jit(solution)/shard_map/ppermute | solution.py:32
  68.5 1.5 collective-permute-done.1
  70.0 1.9 collective-permute-start.9
  72.0 0.5 collective-permute-start.10
  72.4 0.6 collective-permute-done.15
  73.0 0.5 collective-permute-start.6
  73.5 11.5 %collective-permute-done.9.refs_8_ = bf16[512,512]{1,0:T(8,128)(2,1)} collective-permute-done((bf16[512,512]{1,0:T(8,128)(2,1)S(1)}, bf16[512,512]{1,0:T(8,128)(2,1)}, u32[]{:S(2)}, u32[]{:S(2)}) %collective-permute-start.9) | collective-permute-done | bytes 524320 | tf_op jit(solution)/shard_map/ppermute | solution.py:32
  85.0 1.3 collective-permute-start.14
  86.3 8.4 %collective-permute-done.10.refs_9_ = bf16[512,512]{1,0:T(8,128)(2,1)} collective-permute-done((bf16[512,512]{1,0:T(8,128)(2,1)S(1)}, bf16[512,512]{1,0:T(8,128)(2,1)}, u32[]{:S(2)}, u32[]{:S(2)}) %collective-permute-start.10) | collective-permute-done | bytes 524320 | tf_op jit(solution)/shard_map/ppermute | solution.py:32
  94.7 1.4 collective-permute-start.16
  96.1 0.8 copy-done.1
  96.9 0.8 copy-done.3
  97.7 1.5 collective-permute-start.17
  99.2 1.5 collective-permute-start.18
  100.6 0.8 copy-done.5
  101.4 5.0 %collective-permute-start.11 = (bf16[512,512]{1,0:T(8,128)(2,1)}, bf16[512,512]{1,0:T(8,128)(2,1)}, u32[]{:S(2)}, u32[]{:S(2)}) collective-permute-start(bf16[512,512]{1,0:T(8,128)(2,1)} %collective-permute-done.9.refs_8_), channel_id=1, source_target_pairs={{0,4},{1,5},{2,6},{3,7},{4,0},{5,1},{6,2},{7,3},{8,12},{9,13},{10,... | collective-permute-start | bytes 1572872 | tf_op jit(solution)/shard_map/ppermute | solution.py:32
  106.4 0.8 copy-done.7
  107.3 3.9 %collective-permute-start.12 = (bf16[512,512]{1,0:T(8,128)(2,1)}, bf16[512,512]{1,0:T(8,128)(2,1)}, u32[]{:S(2)}, u32[]{:S(2)}) collective-permute-start(bf16[512,512]{1,0:T(8,128)(2,1)} %collective-permute-done.10.refs_9_), channel_id=1, source_target_pairs={{0,4},{1,5},{2,6},{3,7},{4,0},{5,1},{6,2},{7,3},{8,12},{9,13},{10,... | collective-permute-start | bytes 1572872 | tf_op jit(solution)/shard_map/ppermute | solution.py:32
  111.4 1.7 collective-permute-done.12.refs_11_
  113.1 1.0 copy-done.2
  114.1 1.0 copy-done.4
  115.1 1.0 copy-done.6
  116.2 1.0 copy-done.8
  117.2 9.8 %shard_map.37 = bf16[4,8,512,128]{3,2,1,0:T(8,128)(2,1)S(1)} custom-call(s32[10]{0:T(128)S(1)} %pad_add_fusion.table, f32[1,1024]{1,0:T(1,128)S(1)} %bitcast.65, bf16[512,1024]{1,0:T(8,128)(2,1)S(1)} %constant_dynamic-slice_fusion.2.refs_0_, bf16[512,1024]{1,0:T(8,128)(2,1)} %collective-permute-done.2.refs_1_, ...), custom_call_target="tpu_custom_call" | custom-call | flops 4294967296 | bytes 12582912 | tf_op jit(solution)/shard_map/pallas_call | solution.py:108
  127.0 1.9 copy-done
  129.0 1.2 dynamic-slice_bitcast_fusion.7
  130.1 0.7 collective-permute-start.24
  130.9 0.7 collective-permute-start.20
  131.6 3.6 %collective-permute-start.27 = (bf16[4,512,128]{2,1,0:T(8,128)(2,1)}, bf16[4,512,128]{2,1,0:T(8,128)(2,1)S(1)}, u32[]{:S(2)}, u32[]{:S(2)}) collective-permute-start(bf16[4,512,128]{2,1,0:T(8,128)(2,1)} %get-tuple-element.10), channel_id=1, source_target_pairs={{0,1},{5,6},{6,7},{7,12},{9,10},{10,11},{11,0},{12,13},{16,17},{21... | collective-permute-start | bytes 1572872 | tf_op jit(solution)/shard_map/ppermute | solution.py:32
  135.2 1.3 collective-permute-start.30
  136.5 1.2 fusion.5
  137.7 0.7 collective-permute-start.25
  138.5 11.7 %collective-permute-done.27 = bf16[4,512,128]{2,1,0:T(8,128)(2,1)S(1)} collective-permute-done((bf16[4,512,128]{2,1,0:T(8,128)(2,1)}, bf16[4,512,128]{2,1,0:T(8,128)(2,1)S(1)}, u32[]{:S(2)}, u32[]{:S(2)}) %collective-permute-start.27) | collective-permute-done | bytes 524320 | tf_op jit(solution)/shard_map/ppermute | solution.py:32
  150.1 5.6 %collective-permute-done.30 = bf16[4,512,128]{2,1,0:T(8,128)(2,1)S(1)} collective-permute-done((bf16[4,512,128]{2,1,0:T(8,128)(2,1)S(1)}, bf16[4,512,128]{2,1,0:T(8,128)(2,1)S(1)}, u32[]{:S(2)}, u32[]{:S(2)}) %collective-permute-start.30) | collective-permute-done | bytes 524320 | tf_op jit(solution)/shard_map/ppermute | solution.py:32
  155.8 2.9 %fusion.6 = (bf16[4,512,128]{2,1,0:T(8,128)(2,1)S(1)}, bf16[4,512,128]{2,1,0:T(8,128)(2,1)}, bf16[4,512,128]{2,1,0:T(8,128)(2,1)S(1)}, bf16[4,512,128]{2,1,0:T(8,128)(2,1)S(1)}) fusion(bf16[4,512,128]{2,1,0:T(8,128)(2,1)S(1)} %collective-permute-done.25, bf16[4,8,512,128]{3,2,1,0:T(8,128)(2,1)} %copy-done, s32[]{:T(128)S(6)} %select_n.206, s32[]{:T(128)S(6)} %add.262, ...), kind=kLoop, calls=%fused_computation.13 | loop fusion | flops 4194304 | bytes 6291476 | tf_op jit(solution)/shard_map/convert_element_type | solution.py:134
  158.6 0.7 collective-permute-start.21
  159.3 5.2 %collective-permute-start.28 = (bf16[4,512,128]{2,1,0:T(8,128)(2,1)}, bf16[4,512,128]{2,1,0:T(8,128)(2,1)S(1)}, u32[]{:S(2)}, u32[]{:S(2)}) collective-permute-start(bf16[4,512,128]{2,1,0:T(8,128)(2,1)} %get-tuple-element.6), channel_id=1, source_target_pairs={{0,1},{1,2},{6,7},{7,12},{10,11},{11,0},{12,13},{13,14},{16,17},{1... | collective-permute-start | bytes 1572872 | tf_op jit(solution)/shard_map/ppermute | solution.py:32
  164.5 2.1 collective-permute-start.31
  166.6 1.2 fusion.8
  167.8 1.5 collective-permute-start.22
  169.3 2.5 %collective-permute-done.28 = bf16[4,512,128]{2,1,0:T(8,128)(2,1)S(1)} collective-permute-done((bf16[4,512,128]{2,1,0:T(8,128)(2,1)}, bf16[4,512,128]{2,1,0:T(8,128)(2,1)S(1)}, u32[]{:S(2)}, u32[]{:S(2)}) %collective-permute-start.28) | collective-permute-done | bytes 524320 | tf_op jit(solution)/shard_map/ppermute | solution.py:32
  171.8 5.6 %collective-permute-done.31 = bf16[4,512,128]{2,1,0:T(8,128)(2,1)S(1)} collective-permute-done((bf16[4,512,128]{2,1,0:T(8,128)(2,1)S(1)}, bf16[4,512,128]{2,1,0:T(8,128)(2,1)S(1)}, u32[]{:S(2)}, u32[]{:S(2)}) %collective-permute-start.31) | collective-permute-done | bytes 524320 | tf_op jit(solution)/shard_map/ppermute | solution.py:32
  177.4 1.9 fusion.9
  179.4 7.3 %collective-permute-start.32 = (bf16[4,512,128]{2,1,0:T(8,128)(2,1)S(1)}, bf16[4,512,128]{2,1,0:T(8,128)(2,1)S(1)}, u32[]{:S(2)}, u32[]{:S(2)}) collective-permute-start(bf16[4,512,128]{2,1,0:T(8,128)(2,1)S(1)} %get-tuple-element.16), channel_id=1, source_target_pairs={{0,1},{1,2},{6,7},{7,12},{10,11},{11,0},{12,13},{13,14},{16,17},{1... | collective-permute-start | bytes 1572872 | tf_op jit(solution)/shard_map/ppermute | solution.py:32
  186.7 6.6 %collective-permute-start.19 = (bf16[4,512,128]{2,1,0:T(8,128)(2,1)}, bf16[4,512,128]{2,1,0:T(8,128)(2,1)S(1)}, u32[]{:S(2)}, u32[]{:S(2)}) collective-permute-start(bf16[4,512,128]{2,1,0:T(8,128)(2,1)} %get-tuple-element.13), channel_id=1, source_target_pairs={{0,4},{1,5},{2,6},{3,7},{12,8},{13,9},{14,10},{15,11},{16,20},{17,... | collective-permute-start | bytes 1572872 | tf_op jit(solution)/shard_map/ppermute | solution.py:32
  193.3 0.7 collective-permute-start.26
  194.0 1.3 collective-permute-start.23
  195.3 4.8 %collective-permute-start.29 = (bf16[4,512,128]{2,1,0:T(8,128)(2,1)S(1)}, bf16[4,512,128]{2,1,0:T(8,128)(2,1)}, u32[]{:S(2)}, u32[]{:S(2)}) collective-permute-start(bf16[4,512,128]{2,1,0:T(8,128)(2,1)S(1)} %get-tuple-element.15), channel_id=1, source_target_pairs={{0,1},{1,2},{2,3},{7,8},{11,0},{12,9},{13,10},{14,11},{16,17},{17,... | collective-permute-start | bytes 1572872 | tf_op jit(solution)/shard_map/ppermute | solution.py:32
  200.1 1.2 fusion.2
  201.3 2.1 collective-permute-start.33
  203.4 5.7 %collective-permute-done.23 = bf16[4,512,128]{2,1,0:T(8,128)(2,1)} collective-permute-done((bf16[4,512,128]{2,1,0:T(8,128)(2,1)S(1)}, bf16[4,512,128]{2,1,0:T(8,128)(2,1)}, u32[]{:S(2)}, u32[]{:S(2)}) %collective-permute-start.23) | collective-permute-done | bytes 524320 | tf_op jit(solution)/shard_map/ppermute | solution.py:32
  209.0 3.3 %collective-permute-done.33 = bf16[4,512,128]{2,1,0:T(8,128)(2,1)} collective-permute-done((bf16[4,512,128]{2,1,0:T(8,128)(2,1)S(1)}, bf16[4,512,128]{2,1,0:T(8,128)(2,1)}, u32[]{:S(2)}, u32[]{:S(2)}) %collective-permute-start.33) | collective-permute-done | bytes 524320 | tf_op jit(solution)/shard_map/ppermute | solution.py:32
  212.4 2.7 %convert_add_fusion.10 = f32[4,512,128]{2,1,0:T(8,128)} fusion(bf16[4,512,128]{2,1,0:T(8,128)(2,1)S(1)} %collective-permute-done.19, bf16[4,512,128]{2,1,0:T(8,128)(2,1)} %collective-permute-done.29, bf16[4,512,128]{2,1,0:T(8,128)(2,1)} %collective-permute-done.33, bf16[4,512,128]{2,1,0:T(8,128)(2,1)} %collective-permute-done.23, ...), kind=kLoop, calls=%fused_computation.20 | loop fusion | flops 2097152 | bytes 4194314 | tf_op jit(solution)/shard_map/add | solution.py:195
  (44 shorter events, 0.3 us)
Async XLA Ops:
  0.0 59.8 %copy-start.10 = (s32[1,4]{1,0:T(1,128)S(1)}, s32[1,4]{1,0:T(1,128)}, u32[]{:S(2)}) copy-start(s32[1,4]{1,0:T(1,128)} %param.5) | copy-start | bytes 52
  0.0 111.2 %copy-start.9 = (f32[2048]{0:T(1024)S(1)}, f32[2048]{0:T(1024)}, u32[]{:S(2)}) copy-start(f32[2048]{0:T(1024)} %param.4) | copy-start | bytes 24580
  2.3 22.4 %collective-permute-start.3 = (bf16[512,512]{1,0:T(8,128)(2,1)}, bf16[512,512]{1,0:T(8,128)(2,1)S(1)}, u32[]{:S(2)}, u32[]{:S(2)}) collective-permute-start(bf16[512,512]{1,0:T(8,128)(2,1)} %get-tuple-element.20), channel_id=1, source_target_pairs={{0,8},{1,9},{2,10},{3,11},{4,12},{5,13},{6,14},{7,15},{8,0},{9,1},... | collective-permute-start | bytes 1572872 | tf_op jit(solution)/shard_map/ppermute | solution.py:32
  9.5 44.7 %collective-permute-start.4 = (bf16[512,512]{1,0:T(8,128)(2,1)}, bf16[512,512]{1,0:T(8,128)(2,1)S(1)}, u32[]{:S(2)}, u32[]{:S(2)}) collective-permute-start(bf16[512,512]{1,0:T(8,128)(2,1)} %get-tuple-element.19), channel_id=1, source_target_pairs={{0,8},{1,9},{2,10},{3,11},{4,12},{5,13},{6,14},{7,15},{8,0},{9,1},... | collective-permute-start | bytes 1572872 | tf_op jit(solution)/shard_map/ppermute | solution.py:32
  10.8 62.2 %collective-permute-start.7 = (bf16[512,1024]{1,0:T(8,128)(2,1)S(1)}, bf16[512,1024]{1,0:T(8,128)(2,1)S(1)}, u32[]{:S(2)}, u32[]{:S(2)}) collective-permute-start(bf16[512,1024]{1,0:T(8,128)(2,1)S(1)} %constant_dynamic-slice_fusion.2.refs_0_), channel_id=1, source_target_pairs={{0,240},{1,241},{2,242},{3,243},{4,244},{5,245},{6,246},{7,247},{8... | collective-permute-start | bytes 3145736 | tf_op jit(solution)/shard_map/ppermute | solution.py:32
  56.7 15.3 %collective-permute-start.13 = (bf16[512,512]{1,0:T(8,128)(2,1)}, bf16[512,512]{1,0:T(8,128)(2,1)}, u32[]{:S(2)}, u32[]{:S(2)}) collective-permute-start(bf16[512,512]{1,0:T(8,128)(2,1)} %get-tuple-element.18), channel_id=1, source_target_pairs={{0,16},{1,17},{2,18},{3,19},{4,20},{5,21},{6,22},{7,23},{8,24},{9,... | collective-permute-start | bytes 1572872 | tf_op jit(solution)/shard_map/ppermute | solution.py:32
  58.2 14.7 %collective-permute-start.15 = (bf16[512,512]{1,0:T(8,128)(2,1)}, bf16[512,512]{1,0:T(8,128)(2,1)}, u32[]{:S(2)}, u32[]{:S(2)}) collective-permute-start(bf16[512,512]{1,0:T(8,128)(2,1)} %get-tuple-element.17), channel_id=1, source_target_pairs={{0,16},{1,17},{2,18},{3,19},{4,20},{5,21},{6,22},{7,23},{8,24},{9,... | collective-permute-start | bytes 1572872 | tf_op jit(solution)/shard_map/ppermute | solution.py:32
  59.8 39.3 %collective-permute-start.2 = (bf16[512,1024]{1,0:T(8,128)(2,1)S(1)}, bf16[512,1024]{1,0:T(8,128)(2,1)}, u32[]{:S(2)}, u32[]{:S(2)}) collective-permute-start(bf16[512,1024]{1,0:T(8,128)(2,1)S(1)} %constant_dynamic-slice_fusion.2.refs_0_), channel_id=1, source_target_pairs={{0,4},{1,5},{2,6},{3,7},{4,0},{5,1},{6,2},{7,3},{8,12},{9,13},{10,... | collective-permute-start | bytes 3145736 | tf_op jit(solution)/shard_map/ppermute | solution.py:32
  59.8 2.3 %collective-permute-start = (s32[1,4]{1,0:T(1,128)S(1)}, s32[1,4]{1,0:T(1,128)S(1)}, u32[]{:S(2)}, u32[]{:S(2)}) collective-permute-start(s32[1,4]{1,0:T(1,128)S(1)} %and_select_fusion.2), channel_id=1, source_target_pairs={{0,4},{1,5},{2,6},{3,7},{4,0},{5,1},{6,2},{7,3},{8,12},{9,13},{10,... | collective-permute-start | bytes 56 | tf_op jit(solution)/shard_map/ppermute | solution.py:32
  62.1 7.9 %collective-permute-start.1 = (s32[2,4]{1,0:T(2,128)S(1)}, s32[2,4]{1,0:T(2,128)S(1)}, u32[]{:S(2)}, u32[]{:S(2)}) collective-permute-start(s32[2,4]{1,0:T(2,128)S(1)} %add_select_fusion), channel_id=1, source_target_pairs={{0,8},{1,9},{2,10},{3,11},{4,12},{5,13},{6,14},{7,15},{8,0},{9,1},... | collective-permute-start | bytes 104 | tf_op jit(solution)/shard_map/ppermute | solution.py:32
  70.0 15.0 %collective-permute-start.9 = (bf16[512,512]{1,0:T(8,128)(2,1)S(1)}, bf16[512,512]{1,0:T(8,128)(2,1)}, u32[]{:S(2)}, u32[]{:S(2)}) collective-permute-start(bf16[512,512]{1,0:T(8,128)(2,1)S(1)} %collective-permute-done.3.refs_2_), channel_id=1, source_target_pairs={{0,240},{1,241},{2,242},{3,243},{4,244},{5,245},{6,246},{7,247},{8... | collective-permute-start | bytes 1572872 | tf_op jit(solution)/shard_map/ppermute | solution.py:32
  72.0 22.7 %collective-permute-start.10 = (bf16[512,512]{1,0:T(8,128)(2,1)S(1)}, bf16[512,512]{1,0:T(8,128)(2,1)}, u32[]{:S(2)}, u32[]{:S(2)}) collective-permute-start(bf16[512,512]{1,0:T(8,128)(2,1)S(1)} %collective-permute-done.4.refs_3_), channel_id=1, source_target_pairs={{0,240},{1,241},{2,242},{3,243},{4,244},{5,245},{6,246},{7,247},{8... | collective-permute-start | bytes 1572872 | tf_op jit(solution)/shard_map/ppermute | solution.py:32
  73.0 23.1 %collective-permute-start.5 = (bf16[512,512]{1,0:T(8,128)(2,1)S(1)}, bf16[512,512]{1,0:T(8,128)(2,1)S(1)}, u32[]{:S(2)}, u32[]{:S(2)}) collective-permute-start(bf16[512,512]{1,0:T(8,128)(2,1)S(1)} %collective-permute-done.3.refs_2_), channel_id=1, source_target_pairs={{0,4},{1,5},{2,6},{3,7},{4,0},{5,1},{6,2},{7,3},{8,12},{9,13},{10,... | collective-permute-start | bytes 1572872 | tf_op jit(solution)/shard_map/ppermute | solution.py:32
  73.0 23.9 %collective-permute-start.6 = (bf16[512,512]{1,0:T(8,128)(2,1)S(1)}, bf16[512,512]{1,0:T(8,128)(2,1)S(1)}, u32[]{:S(2)}, u32[]{:S(2)}) collective-permute-start(bf16[512,512]{1,0:T(8,128)(2,1)S(1)} %collective-permute-done.4.refs_3_), channel_id=1, source_target_pairs={{0,4},{1,5},{2,6},{3,7},{4,0},{5,1},{6,2},{7,3},{8,12},{9,13},{10,... | collective-permute-start | bytes 1572872 | tf_op jit(solution)/shard_map/ppermute | solution.py:32
  85.0 15.6 %collective-permute-start.14 = (bf16[512,512]{1,0:T(8,128)(2,1)}, bf16[512,512]{1,0:T(8,128)(2,1)S(1)}, u32[]{:S(2)}, u32[]{:S(2)}) collective-permute-start(bf16[512,512]{1,0:T(8,128)(2,1)} %collective-permute-done.13), channel_id=1, source_target_pairs={{0,20},{1,21},{2,22},{3,23},{8,28},{9,29},{10,30},{11,31},{16,228}... | collective-permute-start | bytes 1572872 | tf_op jit(solution)/shard_map/ppermute | solution.py:32
  94.7 11.7 %collective-permute-start.16 = (bf16[512,512]{1,0:T(8,128)(2,1)}, bf16[512,512]{1,0:T(8,128)(2,1)S(1)}, u32[]{:S(2)}, u32[]{:S(2)}) collective-permute-start(bf16[512,512]{1,0:T(8,128)(2,1)} %collective-permute-done.15), channel_id=1, source_target_pairs={{0,20},{1,21},{2,22},{3,23},{8,28},{9,29},{10,30},{11,31},{16,228}... | collective-permute-start | bytes 1572872 | tf_op jit(solution)/shard_map/ppermute | solution.py:32
  96.1 0.8 copy-start.1
  96.9 16.2 %collective-permute-start.8 = (bf16[512,1024]{1,0:T(8,128)(2,1)S(1)}, bf16[512,1024]{1,0:T(8,128)(2,1)}, u32[]{:S(2)}, u32[]{:S(2)}) collective-permute-start(bf16[512,1024]{1,0:T(8,128)(2,1)S(1)} %collective-permute-done.7.refs_6_), channel_id=1, source_target_pairs={{0,4},{1,5},{2,6},{3,7},{4,0},{5,1},{6,2},{7,3},{8,12},{9,13},{10,... | collective-permute-start | bytes 3145736 | tf_op jit(solution)/shard_map/ppermute | solution.py:32
  96.9 0.8 copy-start.3
  97.7 13.7 %collective-permute-start.17 = (bf16[512,512]{1,0:T(8,128)(2,1)}, bf16[512,512]{1,0:T(8,128)(2,1)}, u32[]{:S(2)}, u32[]{:S(2)}) collective-permute-start(bf16[512,512]{1,0:T(8,128)(2,1)} %collective-permute-done.13), channel_id=1, source_target_pairs={{4,20},{5,21},{6,22},{7,23},{12,28},{13,29},{14,30},{15,31},{20,22... | collective-permute-start | bytes 1572872 | tf_op jit(solution)/shard_map/ppermute | solution.py:32
  99.2 12.2 %collective-permute-start.18 = (bf16[512,512]{1,0:T(8,128)(2,1)}, bf16[512,512]{1,0:T(8,128)(2,1)}, u32[]{:S(2)}, u32[]{:S(2)}) collective-permute-start(bf16[512,512]{1,0:T(8,128)(2,1)} %collective-permute-done.15), channel_id=1, source_target_pairs={{4,20},{5,21},{6,22},{7,23},{12,28},{13,29},{14,30},{15,31},{20,22... | collective-permute-start | bytes 1572872 | tf_op jit(solution)/shard_map/ppermute | solution.py:32
  100.6 0.8 copy-start.5
  101.4 10.0 %collective-permute-start.11 = (bf16[512,512]{1,0:T(8,128)(2,1)}, bf16[512,512]{1,0:T(8,128)(2,1)}, u32[]{:S(2)}, u32[]{:S(2)}) collective-permute-start(bf16[512,512]{1,0:T(8,128)(2,1)} %collective-permute-done.9.refs_8_), channel_id=1, source_target_pairs={{0,4},{1,5},{2,6},{3,7},{4,0},{5,1},{6,2},{7,3},{8,12},{9,13},{10,... | collective-permute-start | bytes 1572872 | tf_op jit(solution)/shard_map/ppermute | solution.py:32
  106.4 0.8 copy-start.7
  107.3 5.8 %collective-permute-start.12 = (bf16[512,512]{1,0:T(8,128)(2,1)}, bf16[512,512]{1,0:T(8,128)(2,1)}, u32[]{:S(2)}, u32[]{:S(2)}) collective-permute-start(bf16[512,512]{1,0:T(8,128)(2,1)} %collective-permute-done.10.refs_9_), channel_id=1, source_target_pairs={{0,4},{1,5},{2,6},{3,7},{4,0},{5,1},{6,2},{7,3},{8,12},{9,13},{10,... | collective-permute-start | bytes 1572872 | tf_op jit(solution)/shard_map/ppermute | solution.py:32
  113.1 1.0 copy-start.2
  114.1 1.0 copy-start.4
  115.1 1.0 copy-start.6
  116.2 1.0 copy-start.8
  127.0 2.0 copy-start
  130.1 6.4 %collective-permute-start.24 = (bf16[4,512,128]{2,1,0:T(8,128)(2,1)S(1)}, bf16[4,512,128]{2,1,0:T(8,128)(2,1)S(1)}, u32[]{:S(2)}, u32[]{:S(2)}) collective-permute-start(bf16[4,512,128]{2,1,0:T(8,128)(2,1)S(1)} %get-tuple-element.9), channel_id=1, source_target_pairs={{3,2},{4,15},{5,4},{6,5},{8,3},{9,8},{10,9},{15,14},{19,18},{20,31... | collective-permute-start | bytes 1572872 | tf_op jit(solution)/shard_map/ppermute | solution.py:32
  130.9 7.6 %collective-permute-start.20 = (bf16[4,512,128]{2,1,0:T(8,128)(2,1)}, bf16[4,512,128]{2,1,0:T(8,128)(2,1)S(1)}, u32[]{:S(2)}, u32[]{:S(2)}) collective-permute-start(bf16[4,512,128]{2,1,0:T(8,128)(2,1)} %get-tuple-element.12), channel_id=1, source_target_pairs={{4,15},{5,4},{6,5},{7,6},{8,3},{9,8},{10,9},{11,10},{20,31},{21,20... | collective-permute-start | bytes 1572872 | tf_op jit(solution)/shard_map/ppermute | solution.py:32
  131.6 18.6 %collective-permute-start.27 = (bf16[4,512,128]{2,1,0:T(8,128)(2,1)}, bf16[4,512,128]{2,1,0:T(8,128)(2,1)S(1)}, u32[]{:S(2)}, u32[]{:S(2)}) collective-permute-start(bf16[4,512,128]{2,1,0:T(8,128)(2,1)} %get-tuple-element.10), channel_id=1, source_target_pairs={{0,1},{5,6},{6,7},{7,12},{9,10},{10,11},{11,0},{12,13},{16,17},{21... | collective-permute-start | bytes 1572872 | tf_op jit(solution)/shard_map/ppermute | solution.py:32
  135.2 20.6 %collective-permute-start.30 = (bf16[4,512,128]{2,1,0:T(8,128)(2,1)S(1)}, bf16[4,512,128]{2,1,0:T(8,128)(2,1)S(1)}, u32[]{:S(2)}, u32[]{:S(2)}) collective-permute-start(bf16[4,512,128]{2,1,0:T(8,128)(2,1)S(1)} %get-tuple-element.11), channel_id=1, source_target_pairs={{4,5},{5,6},{6,7},{7,12},{8,9},{9,10},{10,11},{11,0},{20,21},{21,2... | collective-permute-start | bytes 1572872 | tf_op jit(solution)/shard_map/ppermute | solution.py:32
  137.7 18.1 %collective-permute-start.25 = (bf16[4,512,128]{2,1,0:T(8,128)(2,1)S(1)}, bf16[4,512,128]{2,1,0:T(8,128)(2,1)S(1)}, u32[]{:S(2)}, u32[]{:S(2)}) collective-permute-start(bf16[4,512,128]{2,1,0:T(8,128)(2,1)S(1)} %fusion.5), channel_id=1, source_target_pairs={{2,1},{3,2},{4,15},{5,4},{8,3},{9,8},{14,13},{15,14},{18,17},{19,1... | collective-permute-start | bytes 1572872 | tf_op jit(solution)/shard_map/ppermute | solution.py:32
  158.6 7.9 %collective-permute-start.21 = (bf16[4,512,128]{2,1,0:T(8,128)(2,1)S(1)}, bf16[4,512,128]{2,1,0:T(8,128)(2,1)S(1)}, u32[]{:S(2)}, u32[]{:S(2)}) collective-permute-start(bf16[4,512,128]{2,1,0:T(8,128)(2,1)S(1)} %get-tuple-element.7), channel_id=1, source_target_pairs={{3,2},{4,15},{5,4},{6,5},{8,3},{9,8},{10,9},{15,14},{19,18},{20,31... | collective-permute-start | bytes 1572872 | tf_op jit(solution)/shard_map/ppermute | solution.py:32
  159.3 12.5 %collective-permute-start.28 = (bf16[4,512,128]{2,1,0:T(8,128)(2,1)}, bf16[4,512,128]{2,1,0:T(8,128)(2,1)S(1)}, u32[]{:S(2)}, u32[]{:S(2)}) collective-permute-start(bf16[4,512,128]{2,1,0:T(8,128)(2,1)} %get-tuple-element.6), channel_id=1, source_target_pairs={{0,1},{1,2},{6,7},{7,12},{10,11},{11,0},{12,13},{13,14},{16,17},{1... | collective-permute-start | bytes 1572872 | tf_op jit(solution)/shard_map/ppermute | solution.py:32
  164.5 12.9 %collective-permute-start.31 = (bf16[4,512,128]{2,1,0:T(8,128)(2,1)S(1)}, bf16[4,512,128]{2,1,0:T(8,128)(2,1)S(1)}, u32[]{:S(2)}, u32[]{:S(2)}) collective-permute-start(bf16[4,512,128]{2,1,0:T(8,128)(2,1)S(1)} %get-tuple-element.8), channel_id=1, source_target_pairs={{0,1},{5,6},{6,7},{7,12},{9,10},{10,11},{11,0},{12,13},{16,17},{21... | collective-permute-start | bytes 1572872 | tf_op jit(solution)/shard_map/ppermute | solution.py:32
  167.8 9.7 %collective-permute-start.22 = (bf16[4,512,128]{2,1,0:T(8,128)(2,1)S(1)}, bf16[4,512,128]{2,1,0:T(8,128)(2,1)}, u32[]{:S(2)}, u32[]{:S(2)}) collective-permute-start(bf16[4,512,128]{2,1,0:T(8,128)(2,1)S(1)} %fusion.8), channel_id=1, source_target_pairs={{2,1},{3,2},{4,15},{5,4},{8,3},{9,8},{14,13},{15,14},{18,17},{19,1... | collective-permute-start | bytes 1572872 | tf_op jit(solution)/shard_map/ppermute | solution.py:32
  179.4 20.7 %collective-permute-start.32 = (bf16[4,512,128]{2,1,0:T(8,128)(2,1)S(1)}, bf16[4,512,128]{2,1,0:T(8,128)(2,1)S(1)}, u32[]{:S(2)}, u32[]{:S(2)}) collective-permute-start(bf16[4,512,128]{2,1,0:T(8,128)(2,1)S(1)} %get-tuple-element.16), channel_id=1, source_target_pairs={{0,1},{1,2},{6,7},{7,12},{10,11},{11,0},{12,13},{13,14},{16,17},{1... | collective-permute-start | bytes 1572872 | tf_op jit(solution)/shard_map/ppermute | solution.py:32
  186.7 16.7 %collective-permute-start.19 = (bf16[4,512,128]{2,1,0:T(8,128)(2,1)}, bf16[4,512,128]{2,1,0:T(8,128)(2,1)S(1)}, u32[]{:S(2)}, u32[]{:S(2)}) collective-permute-start(bf16[4,512,128]{2,1,0:T(8,128)(2,1)} %get-tuple-element.13), channel_id=1, source_target_pairs={{0,4},{1,5},{2,6},{3,7},{12,8},{13,9},{14,10},{15,11},{16,20},{17,... | collective-permute-start | bytes 1572872 | tf_op jit(solution)/shard_map/ppermute | solution.py:32
  193.3 10.1 %collective-permute-start.26 = (bf16[4,512,128]{2,1,0:T(8,128)(2,1)S(1)}, bf16[4,512,128]{2,1,0:T(8,128)(2,1)S(1)}, u32[]{:S(2)}, u32[]{:S(2)}) collective-permute-start(bf16[4,512,128]{2,1,0:T(8,128)(2,1)S(1)} %get-tuple-element.5), channel_id=1, source_target_pairs={{1,4},{2,5},{3,6},{4,15},{8,7},{13,12},{14,13},{15,14},{17,20},{18... | collective-permute-start | bytes 1572872 | tf_op jit(solution)/shard_map/ppermute | solution.py:32
  194.0 15.1 %collective-permute-start.23 = (bf16[4,512,128]{2,1,0:T(8,128)(2,1)S(1)}, bf16[4,512,128]{2,1,0:T(8,128)(2,1)}, u32[]{:S(2)}, u32[]{:S(2)}) collective-permute-start(bf16[4,512,128]{2,1,0:T(8,128)(2,1)S(1)} %get-tuple-element.14), channel_id=1, source_target_pairs={{1,0},{2,1},{3,2},{4,11},{8,3},{13,8},{14,9},{15,10},{17,16},{18,1... | collective-permute-start | bytes 1572872 | tf_op jit(solution)/shard_map/ppermute | solution.py:32
  195.3 13.8 %collective-permute-start.29 = (bf16[4,512,128]{2,1,0:T(8,128)(2,1)S(1)}, bf16[4,512,128]{2,1,0:T(8,128)(2,1)}, u32[]{:S(2)}, u32[]{:S(2)}) collective-permute-start(bf16[4,512,128]{2,1,0:T(8,128)(2,1)S(1)} %get-tuple-element.15), channel_id=1, source_target_pairs={{0,1},{1,2},{2,3},{7,8},{11,0},{12,9},{13,10},{14,11},{16,17},{17,... | collective-permute-start | bytes 1572872 | tf_op jit(solution)/shard_map/ppermute | solution.py:32
  201.3 11.1 %collective-permute-start.33 = (bf16[4,512,128]{2,1,0:T(8,128)(2,1)S(1)}, bf16[4,512,128]{2,1,0:T(8,128)(2,1)}, u32[]{:S(2)}, u32[]{:S(2)}) collective-permute-start(bf16[4,512,128]{2,1,0:T(8,128)(2,1)S(1)} %fusion.2), channel_id=1, source_target_pairs={{0,5},{1,6},{2,7},{7,12},{11,4},{12,13},{13,14},{14,15},{16,21},{1... | collective-permute-start | bytes 1572872 | tf_op jit(solution)/shard_map/ppermute | solution.py:32

commit v2 on v0

v2 whole, which is shorter than its diff:
```python
import functools

import jax
import jax.numpy as jnp
from jax import lax
from jax.experimental import pallas as pl
from jax.experimental.pallas import tpu as pltpu
from jax.sharding import PartitionSpec as P

SLOTS = 4
TB = 512
WIDE = 1024
WIDTHS = (640, 384)
DEPTH = 4
AXES = ("trans", "pw")


def place(device):
    trans, pw = divmod(device, 4)
    return trans // 16, trans // 4 % 4, trans // 2 % 2 * 4 + pw, trans % 2


def device_at(x, y, z, core):
    z %= 8
    return (((x % 4 * 4 + y % 4) * 2 + z // 4) * 2 + core) * 4 + z % 4


def send(value, target, half=None):
    pairs = []
    for device in range(256):
        x, y, z, core = place(device)
        there = target(x, y, z, core)
        if there is not None and half in (None, z // 4):
            pairs.append((device, device_at(*there)))
    return lax.ppermute(value, AXES, pairs)


def other_half(x, y, z, core):
    return x, y, z + 4, core


def other_core(x, y, z, core):
    return x, y, z, 1 - core


def to_core_1(x, y, z, core):
    return (x, y, z, 1) if core == 0 else None


def previous_column(x, y, z, core):
    column = (x * 4 + y - 1) % 16
    return column // 4, column % 4, z, core


def two_columns_back(x, y, z, core):
    column = (x * 4 + y - 2) % 16
    return column // 4, column % 4, z, core


def up_one(x, y, z, core):
    return x, y + 1, z, core


def up_to_owner(x, y, z, core):
    return (x if y in (3, 0) else x - 1), y + 1, z, core


def tile_kernel(counts, table, *refs):
    total = sum(counts)
    blocks, outs = refs[:total], refs[total : total + 9]
    weighted, held, weighted_sem, sems = refs[total + 9 :]
    groups = []
    at = 0
    for count in counts:
        groups.append(blocks[at : at + count])
        at += count

    def copies(group, target, sem):
        start = 0
        for ref in group:
            width = ref.shape[1]
            pltpu.make_async_copy(ref.at[pl.ds(0, TB)], target.at[:, pl.ds(start, width)], sem).start()
            start += width

    def whole(target, sem):
        pltpu.make_async_copy(target, target, sem).wait()

    def fetch(tile, slot):
        for index, group in enumerate(groups[2:]):

            @pl.when(table[tile] == index)
            def _():
                copies(group, held.at[slot], sems.at[slot])

    half = table[8]
    z = table[9]
    for which in range(2):

        @pl.when(half == which)
        def _():
            copies(groups[which], weighted.at[0], weighted_sem.at[0])

    fetch(0, 0)
    fetch(1, 1)
    for which in range(2):

        @pl.when(half == which)
        def _():
            copies(groups[1 - which], weighted.at[1], weighted_sem.at[1])

    def step(tile, carry):
        owner = tile // SLOTS
        place = tile % SLOTS
        slot = tile % DEPTH

        @pl.when(tile + 2 < 2 * SLOTS)
        def _():
            fetch(tile + 2, (tile + 2) % DEPTH)

        @pl.when(place == 0)
        def _():
            whole(weighted.at[owner], weighted_sem.at[owner])

        whole(held.at[slot], sems.at[slot])
        result = lax.dot_general(
            weighted[owner], held[slot], (((1,), (1,)), ((), ())), preferred_element_type=jnp.float32
        )
        for part in range(4):
            column = result[:, part * 128 : (part + 1) * 128]
            ahead = (owner * 4 + part - z + 8) % 8

            @pl.when(ahead == 0)
            def _():
                outs[0][place] = column

            for distance in (1, 2, 3, 5, 6, 7):

                @pl.when(ahead == distance)
                def _():
                    outs[distance][place] = column.astype(jnp.bfloat16)

            @pl.when((ahead == 4) & (place < 2))
            def _():
                outs[4][place] = column.astype(jnp.bfloat16)

            @pl.when((ahead == 4) & (place >= 2))
            def _():
                outs[8][place - 2] = column.astype(jnp.bfloat16)

        return carry

    lax.fori_loop(0, 2 * SLOTS, step, 0)


def partial_tiles(table, groups):
    counts = [len(group) for group in groups]
    blocks = [piece for group in groups for piece in group]
    shapes = [jax.ShapeDtypeStruct((SLOTS, TB, 128), jnp.float32)]
    for distance in range(1, 9):
        shapes.append(jax.ShapeDtypeStruct((2 if distance in (4, 8) else SLOTS, TB, 128), jnp.bfloat16))
    return pl.pallas_call(
        functools.partial(tile_kernel, counts),
        out_shape=tuple(shapes),
        in_specs=[pl.BlockSpec(memory_space=pltpu.SMEM)] + [pl.BlockSpec(memory_space=pltpu.HBM)] * len(blocks),
        out_specs=tuple(pl.BlockSpec(memory_space=pltpu.VMEM) for _ in shapes),
        scratch_shapes=[
            pltpu.VMEM((2, TB, WIDE), jnp.bfloat16),
            pltpu.VMEM((DEPTH, TB, WIDE), jnp.bfloat16),
            pltpu.SemaphoreType.DMA((2,)),
            pltpu.SemaphoreType.DMA((DEPTH,)),
        ],
        compiler_params=pltpu.CompilerParams(vmem_limit_bytes=60 * 1024 * 1024),
        cost_estimate=pl.CostEstimate(flops=8 * 2 * TB * TB * WIDE, bytes_accessed=15 << 20, transcendentals=0),
    )(table, *blocks)


def together(*values):
    return lax.optimization_barrier(values)


def ring(parts):
    def ahead(x, y, z, core):
        return x, y, z + 1, core

    def behind(x, y, z, core):
        return x, y, z - 1, core

    down, up = together(send(parts[4], behind), send(parts[8], ahead))
    for distance in range(3, 0, -1):
        lower, upper = parts[8 - distance].astype(jnp.float32), parts[distance].astype(jnp.float32)
        if distance == 3:
            down = jnp.concatenate([down, jnp.zeros_like(down)])
            up = jnp.concatenate([jnp.zeros_like(up), up])
        down = (lower + down.astype(jnp.float32)).astype(jnp.bfloat16)
        up = (upper + up.astype(jnp.float32)).astype(jnp.bfloat16)
        down, up = together(down, up)
        down, up = together(send(down, behind), send(up, ahead))
    return parts[0] + down.astype(jnp.float32) + up.astype(jnp.float32)


def body(pair_density, coulomb, partners):
    mine = lax.axis_index("trans")
    pw = lax.axis_index("pw")
    core = mine & 1
    half = (mine >> 1) & 1
    offsets = (partners[0] - mine) & 63
    count = len(WIDTHS)
    starts = [sum(WIDTHS[:i]) for i in range(count)]
    away = [lax.dynamic_slice_in_dim(pair_density, (1 - half) * WIDE + at, width, 1) for at, width in zip(starts, WIDTHS)]
    more = jnp.pad(offsets.astype(jnp.bfloat16)[None, :], ((0, 15), (0, WIDTHS[-1] - SLOTS)))
    away[-1] = jnp.concatenate([away[-1], more])
    keep = lax.dynamic_slice_in_dim(pair_density, half * WIDE, WIDE, 1)
    away[0], keep = together(away[0], keep)
    other = [send(piece, other_half) for piece in away]
    keep_next = send(keep, previous_column)
    keep_last = send(keep, up_one, 0)
    weights = lax.dynamic_slice_in_dim(coulomb, half * WIDE, WIDE, 0)[None, :]

    def weigh(piece, at):
        piece = piece[:TB].astype(jnp.float32)
        return (piece * weights[:, at : at + piece.shape[1]]).astype(jnp.bfloat16)

    weighted = [weigh(keep, 0)]
    other[0], keep_next, keep_last = together(other[0], keep_next, keep_last)
    keep_swap = send(keep, other_core)
    other_next, other_last, other_swap, next_swap, last_swap = [], [], [], [], []
    for i in range(count):
        follow = send(other[i], previous_column)
        last = send(other[i], two_columns_back, 1)
        other_swap.append(send(other[i], other_core))
        weighted.append(weigh(other[i], starts[i]))
        if i == 0:
            keep_last = send(keep_last, up_to_owner, 0)
            keep_next_swap = send(keep_next, other_core)
        else:
            next_swap.append(send(other_next[-1], other_core))
            last_swap.append(send(other_last[-1], to_core_1, 1))
        if i == count - 1:
            far = other[i][TB, :SLOTS].astype(jnp.int32)
            keep_last_swap = send(keep_last, to_core_1, 0)
            far, weighted[-1], follow = together(far, weighted[-1], follow)
        else:
            follow, weighted[-1], weighted[0], keep_last = together(follow, weighted[-1], weighted[0], keep_last)
            other[i + 1], follow, last = together(other[i + 1], follow, last)
        other_next.append(follow)
        other_last.append(last)
    next_swap.append(send(other_next[-1], other_core))
    last_swap.append(send(other_last[-1], to_core_1, 1))
    wanted = jnp.where(half == 0, jnp.stack([offsets, far]), jnp.stack([far, offsets]))
    number = 2 * jnp.arange(2, dtype=jnp.int32)[:, None] + core + wanted
    pair = number >> 1
    low = (number & 1) ^ core
    entry = jnp.where(pair < 4, 2 * (pair ^ half) + low, 8 + 2 * half + low)
    table = jnp.concatenate([entry.reshape(-1), jnp.stack([half, half * 4 + pw])]).astype(jnp.int32)
    groups = [weighted[:1], weighted[1:]]
    groups += [[keep], [keep_swap], other, other_swap, [keep_next], [keep_next_swap], other_next, next_swap]
    groups += [[keep_last], [keep_last_swap], other_last, last_swap]
    return ring(partial_tiles(table, groups))


def solution(mesh):
    placed = (P("trans", "pw"), P("pw"), P("trans", None))
    return jax.shard_map(
        body, mesh=mesh, in_specs=placed, out_specs=P("trans", None, "pw"), check_vma=False
    )
```

time: 441 us -> 177 us (0.40)
  waiting for transfers between devices: 351 us -> 73.7 us
  starting transfers between devices: 53.7 us -> 76.1 us
  between operations: 21 us -> 0.23 us
  Pallas kernels: 0 us -> 12.9 us
  other arithmetic: 3.06 us -> 10.1 us
  matrix products: 5.19 us -> 0 us
    ppermute x6 -> x26, waiting for transfers between devices: 252 us -> 73.7 us  [send(): return lax.ppermute(value, AXES, pairs)]
    reduce_scatter x1 -> x0, waiting for transfers between devices: 98.7 us -> none  [body(): return lax.psum_scatter(tiles, 'pw', scatter_dimension=2, tiled=True)]
    ppermute x6 -> x26, starting transfers between devices: 53.7 us -> 76.1 us  [send(): return lax.ppermute(value, AXES, pairs)]
    pallas_call x0 -> x1, Pallas kernels: none -> 12.9 us  [partial_tiles(): pl.pallas_call(functools.partial(tile_kernel, counts), out_shape=tuple(sh...]
    convert_element_type x0 -> x10, other arithmetic: none -> 7.55 us  [the longest x3 4.11 us: weigh(): return (piece * weights[:, at:at + piece.shape[1]]).astype(jnp.bfloat16)]
    dot_general x4 -> x0, matrix products: 5.19 us -> none  [body(): lax.dot_general(weighted, partner, (((1,), (1,)), ((), ())), preferred_el...]
  transfers between devices with their start and end apart: 7 -> 26, of which waited for: 7 -> 12; matrix products, arithmetic and copies ran while one was open for 2% -> 4% of each run, Pallas kernels for 0% -> 0%
where the time goes in v2:
time: 177 us; the launch traced here: 176 us
  starting transfers between devices  76.1 us (43%)
  waiting for transfers between devices  73.7 us (42%)
  Pallas kernels  12.9 us (7%)
  other arithmetic  10.1 us (6%)
  local copies, waits for them, and re-layouts  3.44 us (2%)
    ppermute x26, starting transfers between devices, send(): return lax.ppermute(value, AXES, pairs)  76.1 us
    ppermute x26, waiting for transfers between devices, send(): return lax.ppermute(value, AXES, pairs)  73.7 us
    pallas_call x1, Pallas kernels, partial_tiles(): pl.pallas_call(functools.partial(tile_kernel, counts), out_shape=tuple(sh...  12.9 us
    convert_element_type x3, other arithmetic, weigh(): return (piece * weights[:, at:at + piece.shape[1]]).astype(jnp.bfloat16)  4.11 us
  transfers between devices with their start and end apart: 26, of which 12 were waited for; matrix products, arithmetic and copies ran while one was open for 4% of the time, Pallas kernels for 0%

profile of v2, /device:TPU:6, one launch (start us, length us, event | category | flops | bytes accessed | tf_op | source)
XLA Modules:
  0.0 176.5 jit_solution(13110437727592229926)
XLA Ops:
  0.0 1.6 copy-done
  1.6 0.1 constant_dynamic-slice_fusion.1
  1.7 0.1 constant_dynamic-slice_fusion.refs_3_
  1.8 3.5 %collective-permute-start.3 = (bf16[512,1024]{1,0:T(8,128)(2,1)S(1)}, bf16[512,1024]{1,0:T(8,128)(2,1)}, u32[]{:S(2)}, u32[]{:S(2)}) collective-permute-start(bf16[512,1024]{1,0:T(8,128)(2,1)S(1)} %constant_dynamic-slice_fusion.refs_3_), channel_id=1, source_target_pairs={{0,16},{1,17},{2,18},{3,19},{4,20},{5,21},{6,22},{7,23},{16,32},{1... | collective-permute-start | bytes 3145736 | tf_op jit(solution)/shard_map/ppermute | solution.py:35
  5.3 2.0 %collective-permute-start.2 = (bf16[512,1024]{1,0:T(8,128)(2,1)S(1)}, bf16[512,1024]{1,0:T(8,128)(2,1)S(1)}, u32[]{:S(2)}, u32[]{:S(2)}) collective-permute-start(bf16[512,1024]{1,0:T(8,128)(2,1)S(1)} %constant_dynamic-slice_fusion.refs_3_), channel_id=1, source_target_pairs={{0,240},{1,241},{2,242},{3,243},{4,244},{5,245},{6,246},{7,247},{8... | collective-permute-start | bytes 3145736 | tf_op jit(solution)/shard_map/ppermute | solution.py:35
  7.3 6.7 %collective-permute-start.1 = (bf16[512,640]{1,0:T(8,128)(2,1)S(1)}, bf16[512,640]{1,0:T(8,128)(2,1)}, u32[]{:S(2)}, u32[]{:S(2)}) collective-permute-start(bf16[512,640]{1,0:T(8,128)(2,1)S(1)} %constant_dynamic-slice_fusion.1), channel_id=1, source_target_pairs={{0,8},{1,9},{2,10},{3,11},{4,12},{5,13},{6,14},{7,15},{8,0},{9,1},... | collective-permute-start | bytes 1966088 | tf_op jit(solution)/shard_map/ppermute | solution.py:35
  14.0 18.0 %collective-permute-done.1.refs_5_ = bf16[512,640]{1,0:T(8,128)(2,1)} collective-permute-done((bf16[512,640]{1,0:T(8,128)(2,1)S(1)}, bf16[512,640]{1,0:T(8,128)(2,1)}, u32[]{:S(2)}, u32[]{:S(2)}) %collective-permute-start.1) | collective-permute-done | bytes 655392 | tf_op jit(solution)/shard_map/ppermute | solution.py:35
  32.0 0.0 collective-permute-done.3
  32.0 0.0 collective-permute-done.2.refs_9_
  32.0 10.5 %collective-permute-start.5 = (bf16[512,1024]{1,0:T(8,128)(2,1)}, bf16[512,1024]{1,0:T(8,128)(2,1)}, u32[]{:S(2)}, u32[]{:S(2)}) collective-permute-start(bf16[512,1024]{1,0:T(8,128)(2,1)} %collective-permute-done.3), channel_id=1, source_target_pairs={{0,16},{1,17},{2,18},{3,19},{4,20},{5,21},{6,22},{7,23},{16,224},{... | collective-permute-start | bytes 3145736 | tf_op jit(solution)/shard_map/ppermute | solution.py:35
  42.5 2.1 %collective-permute-start.4 = (bf16[512,640]{1,0:T(8,128)(2,1)}, bf16[512,640]{1,0:T(8,128)(2,1)}, u32[]{:S(2)}, u32[]{:S(2)}) collective-permute-start(bf16[512,640]{1,0:T(8,128)(2,1)} %collective-permute-done.1.refs_5_), channel_id=1, source_target_pairs={{0,240},{1,241},{2,242},{3,243},{4,244},{5,245},{6,246},{7,247},{8... | collective-permute-start | bytes 1966088 | tf_op jit(solution)/shard_map/ppermute | solution.py:35
  44.5 0.0 collective-permute-start.8
  44.6 0.5 fusion.3
  45.1 1.5 collective-permute-start.6
  46.6 7.0 %collective-permute-start = (bf16[528,384]{1,0:T(8,128)(2,1)S(1)}, bf16[528,384]{1,0:T(8,128)(2,1)S(1)}, u32[]{:S(2)}, u32[]{:S(2)}) collective-permute-start(bf16[528,384]{1,0:T(8,128)(2,1)S(1)} %fusion.1), channel_id=1, source_target_pairs={{0,8},{1,9},{2,10},{3,11},{4,12},{5,13},{6,14},{7,15},{8,0},{9,1},... | collective-permute-start | bytes 1216520 | tf_op jit(solution)/shard_map/ppermute | solution.py:35
  53.7 0.7 dynamic_slice.15
  54.4 0.0 collective-permute-done.4.refs_11_
  54.4 0.0 collective-permute-start.9
  54.4 4.9 %collective-permute-done.5.refs_15_ = bf16[512,1024]{1,0:T(8,128)(2,1)} collective-permute-done((bf16[512,1024]{1,0:T(8,128)(2,1)}, bf16[512,1024]{1,0:T(8,128)(2,1)}, u32[]{:S(2)}, u32[]{:S(2)}) %collective-permute-start.5) | collective-permute-done | bytes 1048608 | tf_op jit(solution)/shard_map/ppermute | solution.py:35
  59.3 0.0 collective-permute-start.11
  59.3 1.2 multiply_convert_fusion.refs_0_
  60.5 2.0 %multiply_convert_fusion.1.refs_1_ = bf16[512,640]{1,0:T(8,128)(2,1)} fusion(bf16[512,640]{1,0:T(8,128)(2,1)} %collective-permute-done.1.refs_5_, f32[640]{0:T(1024)S(1)} %slice_reduce_fusion), kind=kLoop, calls=%fused_computation.1 | loop fusion | flops 983040 | bytes 1313280 | tf_op jit(solution)/shard_map/convert_element_type | solution.py:221
  62.6 8.9 %collective-permute-done.refs_6_ = bf16[528,384]{1,0:T(8,128)(2,1)S(1)} collective-permute-done((bf16[528,384]{1,0:T(8,128)(2,1)S(1)}, bf16[528,384]{1,0:T(8,128)(2,1)S(1)}, u32[]{:S(2)}, u32[]{:S(2)}) %collective-permute-start) | collective-permute-done | bytes 405536 | tf_op jit(solution)/shard_map/ppermute | solution.py:35
  71.5 0.0 collective-permute-done.6.refs_17_
  71.5 0.0 collective-permute-start.7
  71.5 2.3 %collective-permute-start.14 = (bf16[512,1024]{1,0:T(8,128)(2,1)}, bf16[512,1024]{1,0:T(8,128)(2,1)}, u32[]{:S(2)}, u32[]{:S(2)}) collective-permute-start(bf16[512,1024]{1,0:T(8,128)(2,1)} %collective-permute-done.5.refs_15_), channel_id=1, source_target_pairs={{0,4},{1,5},{2,6},{3,7},{16,20},{17,21},{18,22},{19,23},{32,36},{3... | collective-permute-start | bytes 3145736 | tf_op jit(solution)/shard_map/ppermute | solution.py:35
  73.8 0.0 collective-permute-done.8.refs_4_
  73.8 1.4 collective-permute-start.15
  75.2 0.8 multiply_convert_fusion.2.refs_2_
  76.0 0.0 collective-permute-done.11.refs_10_
  76.1 0.5 collective-permute-start.12
  76.6 2.9 %collective-permute-done.7.refs_12_ = bf16[528,384]{1,0:T(8,128)(2,1)} collective-permute-done((bf16[528,384]{1,0:T(8,128)(2,1)S(1)}, bf16[528,384]{1,0:T(8,128)(2,1)}, u32[]{:S(2)}, u32[]{:S(2)}) %collective-permute-start.7) | collective-permute-done | bytes 405536 | tf_op jit(solution)/shard_map/ppermute | solution.py:35
  79.5 1.5 collective-permute-start.16
  81.0 0.0 collective-permute-done.15.refs_18_
  81.0 1.4 collective-permute-start.17
  82.4 0.7 compare_select_fusion
  83.2 0.1 reshape.33
  83.3 0.7 pad_add_fusion.table
  83.9 0.0 collective-permute-done.17.refs_20_
  84.0 0.0 collective-permute-done.14.refs_16_
  84.0 0.8 copy-done.10
  84.8 12.9 %shard_map.37 = (f32[4,512,128]{2,1,0:T(8,128)}, bf16[4,512,128]{2,1,0:T(8,128)(2,1)}, bf16[4,512,128]{2,1,0:T(8,128)(2,1)}, bf16[4,512,128]{2,1,0:T(8,128)(2,1)...) custom-call(s32[10]{0:T(128)} %pad_add_fusion.table, ...), custom_call_target="tpu_custom_call" | custom-call | flops 4294967296 | bytes 15728640 | tf_op jit(solution)/shard_map/pallas_call | solution.py:161
  97.7 29.4 %collective-permute-start.18 = (bf16[2,512,128]{2,1,0:T(8,128)(2,1)}, bf16[2,512,128]{2,1,0:T(8,128)(2,1)S(1)}, u32[]{:S(2)}, u32[]{:S(2)}) collective-permute-start(bf16[2,512,128]{2,1,0:T(8,128)(2,1)} %get-tuple-element.62), channel_id=1, source_target_pairs={{0,11},{1,0},{2,1},{3,2},{4,15},{5,4},{6,5},{7,6},{8,3},{9,8},{10,... | collective-permute-start | bytes 786440 | tf_op jit(solution)/shard_map/ppermute | solution.py:35
  127.1 0.0 collective-permute-start.19
  127.1 5.1 %collective-permute-done.18 = bf16[2,512,128]{2,1,0:T(8,128)(2,1)S(1)} collective-permute-done((bf16[2,512,128]{2,1,0:T(8,128)(2,1)}, bf16[2,512,128]{2,1,0:T(8,128)(2,1)S(1)}, u32[]{:S(2)}, u32[]{:S(2)}) %collective-permute-start.18) | collective-permute-done | bytes 262176 | tf_op jit(solution)/shard_map/ppermute | solution.py:35
  132.2 3.3 %collective-permute-done.19 = bf16[2,512,128]{2,1,0:T(8,128)(2,1)S(1)} collective-permute-done((bf16[2,512,128]{2,1,0:T(8,128)(2,1)}, bf16[2,512,128]{2,1,0:T(8,128)(2,1)S(1)}, u32[]{:S(2)}, u32[]{:S(2)}) %collective-permute-start.19) | collective-permute-done | bytes 262176 | tf_op jit(solution)/shard_map/ppermute | solution.py:35
  135.5 1.2 add_convert_fusion.5
  136.7 1.2 add_convert_fusion.4
  137.9 0.4 collective-permute-start.20
  138.2 1.7 collective-permute-start.21
  140.0 9.6 %collective-permute-done.20 = bf16[4,512,128]{2,1,0:T(8,128)(2,1)S(1)} collective-permute-done((bf16[4,512,128]{2,1,0:T(8,128)(2,1)S(1)}, bf16[4,512,128]{2,1,0:T(8,128)(2,1)S(1)}, u32[]{:S(2)}, u32[]{:S(2)}) %collective-permute-start.20) | collective-permute-done | bytes 524320 | tf_op jit(solution)/shard_map/ppermute | solution.py:35
  149.6 1.5 collective-permute-done.21
  151.1 0.1 add_convert_fusion.3
  151.3 0.1 add_convert_fusion.2
  151.4 0.4 collective-permute-start.22
  151.8 1.7 collective-permute-start.23
  153.5 8.7 %collective-permute-done.22 = bf16[4,512,128]{2,1,0:T(8,128)(2,1)S(1)} collective-permute-done((bf16[4,512,128]{2,1,0:T(8,128)(2,1)S(1)}, bf16[4,512,128]{2,1,0:T(8,128)(2,1)S(1)}, u32[]{:S(2)}, u32[]{:S(2)}) %collective-permute-start.22) | collective-permute-done | bytes 524320 | tf_op jit(solution)/shard_map/ppermute | solution.py:35
  162.2 1.5 collective-permute-done.23
  163.7 0.3 add_convert_fusion
  164.0 0.4 collective-permute-start.24
  164.4 1.7 collective-permute-start.25
  166.1 7.8 %collective-permute-done.24 = bf16[4,512,128]{2,1,0:T(8,128)(2,1)S(1)} collective-permute-done((bf16[4,512,128]{2,1,0:T(8,128)(2,1)S(1)}, bf16[4,512,128]{2,1,0:T(8,128)(2,1)S(1)}, u32[]{:S(2)}, u32[]{:S(2)}) %collective-permute-start.24) | collective-permute-done | bytes 524320 | tf_op jit(solution)/shard_map/ppermute | solution.py:35
  173.9 1.5 collective-permute-done.25
  175.4 1.1 convert_add_fusion
  (35 shorter events, 0.2 us)
Async XLA Ops:
  0.0 1.6 copy-start
  0.0 44.5 %copy-start.8 = (s32[1,4]{1,0:T(1,128)S(1)}, s32[1,4]{1,0:T(1,128)}, u32[]{:S(2)}) copy-start(s32[1,4]{1,0:T(1,128)} %param.5) | copy-start | bytes 52
  1.8 60.8 %copy-start.1 = (bf16[512,1024]{1,0:T(8,128)(2,1)}, bf16[512,1024]{1,0:T(8,128)(2,1)S(1)}, u32[]{:S(2)}) copy-start(bf16[512,1024]{1,0:T(8,128)(2,1)S(1)} %constant_dynamic-slice_fusion.refs_3_) | copy-start | bytes 3145732
  1.8 30.2 %collective-permute-start.3 = (bf16[512,1024]{1,0:T(8,128)(2,1)S(1)}, bf16[512,1024]{1,0:T(8,128)(2,1)}, u32[]{:S(2)}, u32[]{:S(2)}) collective-permute-start(bf16[512,1024]{1,0:T(8,128)(2,1)S(1)} %constant_dynamic-slice_fusion.refs_3_), channel_id=1, source_target_pairs={{0,16},{1,17},{2,18},{3,19},{4,20},{5,21},{6,22},{7,23},{16,32},{1... | collective-permute-start | bytes 3145736 | tf_op jit(solution)/shard_map/ppermute | solution.py:35
  5.3 26.7 %collective-permute-start.2 = (bf16[512,1024]{1,0:T(8,128)(2,1)S(1)}, bf16[512,1024]{1,0:T(8,128)(2,1)S(1)}, u32[]{:S(2)}, u32[]{:S(2)}) collective-permute-start(bf16[512,1024]{1,0:T(8,128)(2,1)S(1)} %constant_dynamic-slice_fusion.refs_3_), channel_id=1, source_target_pairs={{0,240},{1,241},{2,242},{3,243},{4,244},{5,245},{6,246},{7,247},{8... | collective-permute-start | bytes 3145736 | tf_op jit(solution)/shard_map/ppermute | solution.py:35
  7.3 24.7 %collective-permute-start.1 = (bf16[512,640]{1,0:T(8,128)(2,1)S(1)}, bf16[512,640]{1,0:T(8,128)(2,1)}, u32[]{:S(2)}, u32[]{:S(2)}) collective-permute-start(bf16[512,640]{1,0:T(8,128)(2,1)S(1)} %constant_dynamic-slice_fusion.1), channel_id=1, source_target_pairs={{0,8},{1,9},{2,10},{3,11},{4,12},{5,13},{6,14},{7,15},{8,0},{9,1},... | collective-permute-start | bytes 1966088 | tf_op jit(solution)/shard_map/ppermute | solution.py:35
  32.0 10.5 %copy-start.9 = (bf16[512,1024]{1,0:T(8,128)(2,1)}, bf16[512,1024]{1,0:T(8,128)(2,1)S(1)}, u32[]{:S(2)}) copy-start(bf16[512,1024]{1,0:T(8,128)(2,1)S(1)} %collective-permute-done.2.refs_9_) | copy-start | bytes 3145732
  32.0 27.3 %collective-permute-start.5 = (bf16[512,1024]{1,0:T(8,128)(2,1)}, bf16[512,1024]{1,0:T(8,128)(2,1)}, u32[]{:S(2)}, u32[]{:S(2)}) collective-permute-start(bf16[512,1024]{1,0:T(8,128)(2,1)} %collective-permute-done.3), channel_id=1, source_target_pairs={{0,16},{1,17},{2,18},{3,19},{4,20},{5,21},{6,22},{7,23},{16,224},{... | collective-permute-start | bytes 3145736 | tf_op jit(solution)/shard_map/ppermute | solution.py:35
  42.5 11.9 %collective-permute-start.4 = (bf16[512,640]{1,0:T(8,128)(2,1)}, bf16[512,640]{1,0:T(8,128)(2,1)}, u32[]{:S(2)}, u32[]{:S(2)}) collective-permute-start(bf16[512,640]{1,0:T(8,128)(2,1)} %collective-permute-done.1.refs_5_), channel_id=1, source_target_pairs={{0,240},{1,241},{2,242},{3,243},{4,244},{5,245},{6,246},{7,247},{8... | collective-permute-start | bytes 1966088 | tf_op jit(solution)/shard_map/ppermute | solution.py:35
  44.5 29.2 %collective-permute-start.8 = (bf16[512,1024]{1,0:T(8,128)(2,1)S(1)}, bf16[512,1024]{1,0:T(8,128)(2,1)}, u32[]{:S(2)}, u32[]{:S(2)}) collective-permute-start(bf16[512,1024]{1,0:T(8,128)(2,1)S(1)} %constant_dynamic-slice_fusion.refs_3_), channel_id=1, source_target_pairs={{0,4},{1,5},{2,6},{3,7},{4,0},{5,1},{6,2},{7,3},{8,12},{9,13},{10,... | collective-permute-start | bytes 3145736 | tf_op jit(solution)/shard_map/ppermute | solution.py:35
  45.1 26.4 %collective-permute-start.6 = (bf16[512,640]{1,0:T(8,128)(2,1)}, bf16[512,640]{1,0:T(8,128)(2,1)}, u32[]{:S(2)}, u32[]{:S(2)}) collective-permute-start(bf16[512,640]{1,0:T(8,128)(2,1)} %collective-permute-done.1.refs_5_), channel_id=1, source_target_pairs={{8,232},{9,233},{10,234},{11,235},{12,236},{13,237},{14,238},{15,2... | collective-permute-start | bytes 1966088 | tf_op jit(solution)/shard_map/ppermute | solution.py:35
  46.6 24.8 %collective-permute-start = (bf16[528,384]{1,0:T(8,128)(2,1)S(1)}, bf16[528,384]{1,0:T(8,128)(2,1)S(1)}, u32[]{:S(2)}, u32[]{:S(2)}) collective-permute-start(bf16[528,384]{1,0:T(8,128)(2,1)S(1)} %fusion.1), channel_id=1, source_target_pairs={{0,8},{1,9},{2,10},{3,11},{4,12},{5,13},{6,14},{7,15},{8,0},{9,1},... | collective-permute-start | bytes 1216520 | tf_op jit(solution)/shard_map/ppermute | solution.py:35
  54.4 20.8 %collective-permute-start.9 = (bf16[512,640]{1,0:T(8,128)(2,1)}, bf16[512,640]{1,0:T(8,128)(2,1)}, u32[]{:S(2)}, u32[]{:S(2)}) collective-permute-start(bf16[512,640]{1,0:T(8,128)(2,1)} %collective-permute-done.1.refs_5_), channel_id=1, source_target_pairs={{0,4},{1,5},{2,6},{3,7},{4,0},{5,1},{6,2},{7,3},{8,12},{9,13},{10,... | collective-permute-start | bytes 1966088 | tf_op jit(solution)/shard_map/ppermute | solution.py:35
  59.3 16.8 %collective-permute-start.11 = (bf16[512,1024]{1,0:T(8,128)(2,1)}, bf16[512,1024]{1,0:T(8,128)(2,1)}, u32[]{:S(2)}, u32[]{:S(2)}) collective-permute-start(bf16[512,1024]{1,0:T(8,128)(2,1)} %copy-done.9), channel_id=1, source_target_pairs={{0,4},{1,5},{2,6},{3,7},{4,0},{5,1},{6,2},{7,3},{8,12},{9,13},{10,... | collective-permute-start | bytes 3145736 | tf_op jit(solution)/shard_map/ppermute | solution.py:35
  71.4 12.5 %copy-start.7 = (bf16[528,384]{1,0:T(8,128)(2,1)}, bf16[528,384]{1,0:T(8,128)(2,1)S(1)}, u32[]{:S(2)}) copy-start(bf16[528,384]{1,0:T(8,128)(2,1)S(1)} %collective-permute-done.refs_6_) | copy-start | bytes 1216516
  71.5 8.0 %collective-permute-start.7 = (bf16[528,384]{1,0:T(8,128)(2,1)S(1)}, bf16[528,384]{1,0:T(8,128)(2,1)}, u32[]{:S(2)}, u32[]{:S(2)}) collective-permute-start(bf16[528,384]{1,0:T(8,128)(2,1)S(1)} %collective-permute-done.refs_6_), channel_id=1, source_target_pairs={{0,240},{1,241},{2,242},{3,243},{4,244},{5,245},{6,246},{7,247},{8... | collective-permute-start | bytes 1216520 | tf_op jit(solution)/shard_map/ppermute | solution.py:35
  71.5 12.5 %collective-permute-start.14 = (bf16[512,1024]{1,0:T(8,128)(2,1)}, bf16[512,1024]{1,0:T(8,128)(2,1)}, u32[]{:S(2)}, u32[]{:S(2)}) collective-permute-start(bf16[512,1024]{1,0:T(8,128)(2,1)} %collective-permute-done.5.refs_15_), channel_id=1, source_target_pairs={{0,4},{1,5},{2,6},{3,7},{16,20},{17,21},{18,22},{19,23},{32,36},{3... | collective-permute-start | bytes 3145736 | tf_op jit(solution)/shard_map/ppermute | solution.py:35
  73.8 7.2 %collective-permute-start.15 = (bf16[528,384]{1,0:T(8,128)(2,1)S(1)}, bf16[528,384]{1,0:T(8,128)(2,1)}, u32[]{:S(2)}, u32[]{:S(2)}) collective-permute-start(bf16[528,384]{1,0:T(8,128)(2,1)S(1)} %collective-permute-done.refs_6_), channel_id=1, source_target_pairs={{8,232},{9,233},{10,234},{11,235},{12,236},{13,237},{14,238},{15,2... | collective-permute-start | bytes 1216520 | tf_op jit(solution)/shard_map/ppermute | solution.py:35
  75.2 5.8 %collective-permute-start.10 = (bf16[528,384]{1,0:T(8,128)(2,1)S(1)}, bf16[528,384]{1,0:T(8,128)(2,1)S(1)}, u32[]{:S(2)}, u32[]{:S(2)}) collective-permute-start(bf16[528,384]{1,0:T(8,128)(2,1)S(1)} %collective-permute-done.refs_6_), channel_id=1, source_target_pairs={{0,4},{1,5},{2,6},{3,7},{4,0},{5,1},{6,2},{7,3},{8,12},{9,13},{10,... | collective-permute-start | bytes 1216520 | tf_op jit(solution)/shard_map/ppermute | solution.py:35
  76.1 7.9 %collective-permute-start.12 = (bf16[512,640]{1,0:T(8,128)(2,1)}, bf16[512,640]{1,0:T(8,128)(2,1)S(1)}, u32[]{:S(2)}, u32[]{:S(2)}) collective-permute-start(bf16[512,640]{1,0:T(8,128)(2,1)} %collective-permute-done.4.refs_11_), channel_id=1, source_target_pairs={{0,4},{1,5},{2,6},{3,7},{4,0},{5,1},{6,2},{7,3},{8,12},{9,13},{10,... | collective-permute-start | bytes 1966088 | tf_op jit(solution)/shard_map/ppermute | solution.py:35
  79.5 4.5 %collective-permute-start.16 = (bf16[512,640]{1,0:T(8,128)(2,1)}, bf16[512,640]{1,0:T(8,128)(2,1)}, u32[]{:S(2)}, u32[]{:S(2)}) collective-permute-start(bf16[512,640]{1,0:T(8,128)(2,1)} %collective-permute-done.6.refs_17_), channel_id=1, source_target_pairs={{8,12},{9,13},{10,14},{11,15},{24,28},{25,29},{26,30},{27,31},{40,... | collective-permute-start | bytes 1966088 | tf_op jit(solution)/shard_map/ppermute | solution.py:35
  81.0 3.0 %collective-permute-start.13 = (bf16[528,384]{1,0:T(8,128)(2,1)}, bf16[528,384]{1,0:T(8,128)(2,1)}, u32[]{:S(2)}, u32[]{:S(2)}) collective-permute-start(bf16[528,384]{1,0:T(8,128)(2,1)} %collective-permute-done.7.refs_12_), channel_id=1, source_target_pairs={{0,4},{1,5},{2,6},{3,7},{4,0},{5,1},{6,2},{7,3},{8,12},{9,13},{10,... | collective-permute-start | bytes 1216520 | tf_op jit(solution)/shard_map/ppermute | solution.py:35
  81.0 1.5 copy-start.11
  81.0 2.9 %collective-permute-start.17 = (bf16[528,384]{1,0:T(8,128)(2,1)}, bf16[528,384]{1,0:T(8,128)(2,1)}, u32[]{:S(2)}, u32[]{:S(2)}) collective-permute-start(bf16[528,384]{1,0:T(8,128)(2,1)} %collective-permute-done.15.refs_18_), channel_id=1, source_target_pairs={{8,12},{9,13},{10,14},{11,15},{24,28},{25,29},{26,30},{27,31},{40,... | collective-permute-start | bytes 1216520 | tf_op jit(solution)/shard_map/ppermute | solution.py:35
  83.9 0.8 copy-start.10
  97.7 53.4 %copy-start.4 = (bf16[4,512,128]{2,1,0:T(8,128)(2,1)S(1)}, bf16[4,512,128]{2,1,0:T(8,128)(2,1)}, u32[]{:S(2)}) copy-start(bf16[4,512,128]{2,1,0:T(8,128)(2,1)} %get-tuple-element.60) | copy-start | bytes 1572868
  97.7 34.4 %collective-permute-start.18 = (bf16[2,512,128]{2,1,0:T(8,128)(2,1)}, bf16[2,512,128]{2,1,0:T(8,128)(2,1)S(1)}, u32[]{:S(2)}, u32[]{:S(2)}) collective-permute-start(bf16[2,512,128]{2,1,0:T(8,128)(2,1)} %get-tuple-element.62), channel_id=1, source_target_pairs={{0,11},{1,0},{2,1},{3,2},{4,15},{5,4},{6,5},{7,6},{8,3},{9,8},{10,... | collective-permute-start | bytes 786440 | tf_op jit(solution)/shard_map/ppermute | solution.py:35
  127.1 8.4 %collective-permute-start.19 = (bf16[2,512,128]{2,1,0:T(8,128)(2,1)}, bf16[2,512,128]{2,1,0:T(8,128)(2,1)S(1)}, u32[]{:S(2)}, u32[]{:S(2)}) collective-permute-start(bf16[2,512,128]{2,1,0:T(8,128)(2,1)} %get-tuple-element.63), channel_id=1, source_target_pairs={{0,1},{1,2},{2,3},{3,8},{4,5},{5,6},{6,7},{7,12},{8,9},{9,10},{10,... | collective-permute-start | bytes 786440 | tf_op jit(solution)/shard_map/ppermute | solution.py:35
  135.5 15.8 %copy-start.3 = (bf16[4,512,128]{2,1,0:T(8,128)(2,1)S(1)}, bf16[4,512,128]{2,1,0:T(8,128)(2,1)}, u32[]{:S(2)}) copy-start(bf16[4,512,128]{2,1,0:T(8,128)(2,1)} %get-tuple-element.70) | copy-start | bytes 1572868
  136.7 27.1 %copy-start.5 = (bf16[4,512,128]{2,1,0:T(8,128)(2,1)S(1)}, bf16[4,512,128]{2,1,0:T(8,128)(2,1)}, u32[]{:S(2)}) copy-start(bf16[4,512,128]{2,1,0:T(8,128)(2,1)} %get-tuple-element.75) | copy-start | bytes 1572868
  136.7 27.0 %copy-start.6 = (bf16[4,512,128]{2,1,0:T(8,128)(2,1)S(1)}, bf16[4,512,128]{2,1,0:T(8,128)(2,1)}, u32[]{:S(2)}) copy-start(bf16[4,512,128]{2,1,0:T(8,128)(2,1)} %get-tuple-element.59) | copy-start | bytes 1572868
  137.9 11.7 %collective-permute-start.20 = (bf16[4,512,128]{2,1,0:T(8,128)(2,1)S(1)}, bf16[4,512,128]{2,1,0:T(8,128)(2,1)S(1)}, u32[]{:S(2)}, u32[]{:S(2)}) collective-permute-start(bf16[4,512,128]{2,1,0:T(8,128)(2,1)S(1)} %add_convert_fusion.5), channel_id=1, source_target_pairs={{0,11},{1,0},{2,1},{3,2},{4,15},{5,4},{6,5},{7,6},{8,3},{9,8},{10,... | collective-permute-start | bytes 1572872 | tf_op jit(solution)/shard_map/ppermute | solution.py:35
  138.2 12.9 %collective-permute-start.21 = (bf16[4,512,128]{2,1,0:T(8,128)(2,1)S(1)}, bf16[4,512,128]{2,1,0:T(8,128)(2,1)S(1)}, u32[]{:S(2)}, u32[]{:S(2)}) collective-permute-start(bf16[4,512,128]{2,1,0:T(8,128)(2,1)S(1)} %add_convert_fusion.4), channel_id=1, source_target_pairs={{0,1},{1,2},{2,3},{3,8},{4,5},{5,6},{6,7},{7,12},{8,9},{9,10},{10,... | collective-permute-start | bytes 1572872 | tf_op jit(solution)/shard_map/ppermute | solution.py:35
  151.3 24.1 %copy-start.2 = (f32[4,512,128]{2,1,0:T(8,128)S(1)}, f32[4,512,128]{2,1,0:T(8,128)}, u32[]{:S(2)}) copy-start(f32[4,512,128]{2,1,0:T(8,128)} %get-tuple-element.58) | copy-start | bytes 3145732
  151.4 10.8 %collective-permute-start.22 = (bf16[4,512,128]{2,1,0:T(8,128)(2,1)S(1)}, bf16[4,512,128]{2,1,0:T(8,128)(2,1)S(1)}, u32[]{:S(2)}, u32[]{:S(2)}) collective-permute-start(bf16[4,512,128]{2,1,0:T(8,128)(2,1)S(1)} %add_convert_fusion.3), channel_id=1, source_target_pairs={{0,11},{1,0},{2,1},{3,2},{4,15},{5,4},{6,5},{7,6},{8,3},{9,8},{10,... | collective-permute-start | bytes 1572872 | tf_op jit(solution)/shard_map/ppermute | solution.py:35
  151.8 11.9 %collective-permute-start.23 = (bf16[4,512,128]{2,1,0:T(8,128)(2,1)S(1)}, bf16[4,512,128]{2,1,0:T(8,128)(2,1)S(1)}, u32[]{:S(2)}, u32[]{:S(2)}) collective-permute-start(bf16[4,512,128]{2,1,0:T(8,128)(2,1)S(1)} %add_convert_fusion.2), channel_id=1, source_target_pairs={{0,1},{1,2},{2,3},{3,8},{4,5},{5,6},{6,7},{7,12},{8,9},{9,10},{10,... | collective-permute-start | bytes 1572872 | tf_op jit(solution)/shard_map/ppermute | solution.py:35
  164.0 9.9 %collective-permute-start.24 = (bf16[4,512,128]{2,1,0:T(8,128)(2,1)S(1)}, bf16[4,512,128]{2,1,0:T(8,128)(2,1)S(1)}, u32[]{:S(2)}, u32[]{:S(2)}) collective-permute-start(bf16[4,512,128]{2,1,0:T(8,128)(2,1)S(1)} %get-tuple-element.77), channel_id=1, source_target_pairs={{0,11},{1,0},{2,1},{3,2},{4,15},{5,4},{6,5},{7,6},{8,3},{9,8},{10,... | collective-permute-start | bytes 1572872 | tf_op jit(solution)/shard_map/ppermute | solution.py:35
  164.4 11.0 %collective-permute-start.25 = (bf16[4,512,128]{2,1,0:T(8,128)(2,1)S(1)}, bf16[4,512,128]{2,1,0:T(8,128)(2,1)S(1)}, u32[]{:S(2)}, u32[]{:S(2)}) collective-permute-start(bf16[4,512,128]{2,1,0:T(8,128)(2,1)S(1)} %get-tuple-element.78), channel_id=1, source_target_pairs={{0,1},{1,2},{2,3},{3,8},{4,5},{5,6},{6,7},{7,12},{8,9},{9,10},{10,... | collective-permute-start | bytes 1572872 | tf_op jit(solution)/shard_map/ppermute | solution.py:35

commit v3 on v2

--- a/solution.py
+++ b/solution.py
@@ -67,8 +67,8 @@
 
 def tile_kernel(counts, table, *refs):
     total = sum(counts)
-    blocks, outs = refs[:total], refs[total : total + 9]
-    weighted, held, weighted_sem, sems = refs[total + 9 :]
+    blocks = refs[:total]
+    out, weighted, held, weighted_sem, sems = refs[total:]
     groups = []
     at = 0
     for count in counts:
@@ -129,23 +129,7 @@
             column = result[:, part * 128 : (part + 1) * 128]
             ahead = (owner * 4 + part - z + 8) % 8
 
-            @pl.when(ahead == 0)
-            def _():
-                outs[0][place] = column
-
-            for distance in (1, 2, 3, 5, 6, 7):
-
-                @pl.when(ahead == distance)
-                def _():
-                    outs[distance][place] = column.astype(jnp.bfloat16)
-
-            @pl.when((ahead == 4) & (place < 2))
-            def _():
-                outs[4][place] = column.astype(jnp.bfloat16)
-
-            @pl.when((ahead == 4) & (place >= 2))
-            def _():
-                outs[8][place - 2] = column.astype(jnp.bfloat16)
+            out[ahead, place] = column.astype(jnp.bfloat16)
 
         return carry
 
@@ -155,14 +139,11 @@
 def partial_tiles(table, groups):
     counts = [len(group) for group in groups]
     blocks = [piece for group in groups for piece in group]
-    shapes = [jax.ShapeDtypeStruct((SLOTS, TB, 128), jnp.float32)]
-    for distance in range(1, 9):
-        shapes.append(jax.ShapeDtypeStruct((2 if distance in (4, 8) else SLOTS, TB, 128), jnp.bfloat16))
     return pl.pallas_call(
         functools.partial(tile_kernel, counts),
-        out_shape=tuple(shapes),
+        out_shape=jax.ShapeDtypeStruct((8, SLOTS, TB, 128), jnp.bfloat16),
         in_specs=[pl.BlockSpec(memory_space=pltpu.SMEM)] + [pl.BlockSpec(memory_space=pltpu.HBM)] * len(blocks),
-        out_specs=tuple(pl.BlockSpec(memory_space=pltpu.VMEM) for _ in shapes),
+        out_specs=pl.BlockSpec(memory_space=pltpu.VMEM),
         scratch_shapes=[
             pltpu.VMEM((2, TB, WIDE), jnp.bfloat16),
             pltpu.VMEM((DEPTH, TB, WIDE), jnp.bfloat16),
@@ -185,7 +166,7 @@
     def behind(x, y, z, core):
         return x, y, z - 1, core
 
-    down, up = together(send(parts[4], behind), send(parts[8], ahead))
+    down, up = together(send(parts[4, :2], behind), send(parts[4, 2:], ahead))
     for distance in range(3, 0, -1):
         lower, upper = parts[8 - distance].astype(jnp.float32), parts[distance].astype(jnp.float32)
         if distance == 3:
@@ -195,7 +176,7 @@
         up = (upper + up.astype(jnp.float32)).astype(jnp.bfloat16)
         down, up = together(down, up)
         down, up = together(send(down, behind), send(up, ahead))
-    return parts[0] + down.astype(jnp.float32) + up.astype(jnp.float32)
+    return parts[0].astype(jnp.float32) + down.astype(jnp.float32) + up.astype(jnp.float32)
 
 
 def body(pair_density, coulomb, partners):
@@ -211,7 +192,7 @@
     away[-1] = jnp.concatenate([away[-1], more])
     keep = lax.dynamic_slice_in_dim(pair_density, half * WIDE, WIDE, 1)
     away[0], keep = together(away[0], keep)
-    other = [send(piece, other_half) for piece in away]
+    other = [send(away[0], other_half)]
     keep_next = send(keep, previous_column)
     keep_last = send(keep, up_one, 0)
     weights = lax.dynamic_slice_in_dim(coulomb, half * WIDE, WIDE, 0)[None, :]
@@ -221,12 +202,15 @@
         return (piece * weights[:, at : at + piece.shape[1]]).astype(jnp.bfloat16)
 
     weighted = [weigh(keep, 0)]
-    other[0], keep_next, keep_last = together(other[0], keep_next, keep_last)
+    other[0], keep_next, keep_last, away[1] = together(other[0], keep_next, keep_last, away[1])
+    other.append(send(away[1], other_half))
     keep_swap = send(keep, other_core)
     other_next, other_last, other_swap, next_swap, last_swap = [], [], [], [], []
     for i in range(count):
         follow = send(other[i], previous_column)
-        last = send(other[i], two_columns_back, 1)
+        last = send(other[i], two_columns_back if i == count - 1 else up_one, 1)
+        if i == count - 1:
+            other_last[-1] = send(other_last[-1], up_to_owner, 1)
         other_swap.append(send(other[i], other_core))
         weighted.append(weigh(other[i], starts[i]))
         if i == 0:
@@ -240,7 +224,8 @@
             keep_last_swap = send(keep_last, to_core_1, 0)
             far, weighted[-1], follow = together(far, weighted[-1], follow)
         else:
-            follow, weighted[-1], weighted[0], keep_last = together(follow, weighted[-1], weighted[0], keep_last)
+            done = (follow, weighted[-1], weighted[0], keep_last, keep_swap, keep_next_swap, other_swap[-1])
+            follow, weighted[-1], weighted[0], keep_last, keep_swap, keep_next_swap, other_swap[-1] = together(*done)
             other[i + 1], follow, last = together(other[i + 1], follow, last)
         other_next.append(follow)
         other_last.append(last)

time: 177 us -> 178 us (level)
  other arithmetic: 10.1 us -> 13.2 us
  local copies, waits for them, and re-layouts: 3.44 us -> 6.1 us
  Pallas kernels: 12.9 us -> 11 us
  starting transfers between devices: 76.1 us -> 74.3 us
    convert_element_type x3, other arithmetic: 1.62 us -> 4.33 us  [ring(): up = (upper + up.astype(jnp.float32)).astype(jnp.bfloat16)]
    pallas_call x1, Pallas kernels: 12.9 us -> 11 us  [partial_tiles(): pl.pallas_call(functools.partial(tile_kernel, counts), out_shape=jax.Shap...]
    ppermute x26 -> x27, starting transfers between devices: 76.1 us -> 74.3 us  [send(): return lax.ppermute(value, AXES, pairs)]
    ppermute x26 -> x27, waiting for transfers between devices: 73.7 us -> 72.6 us  [send(): return lax.ppermute(value, AXES, pairs)]
  transfers between devices with their start and end apart: 26 -> 27, of which waited for: 12 -> 12; matrix products, arithmetic and copies ran while one was open for 4% -> 4% of each run, Pallas kernels for 0% -> 0%
where the time goes in v3:
time: 178 us; the launch traced here: 177 us
  starting transfers between devices  74.3 us (42%)
  waiting for transfers between devices  72.6 us (41%)
  other arithmetic  13.2 us (7%)
  Pallas kernels  11 us (6%)
  local copies, waits for them, and re-layouts  6.1 us (3%)
    ppermute x27, starting transfers between devices, send(): return lax.ppermute(value, AXES, pairs)  74.3 us
    ppermute x27, waiting for transfers between devices, send(): return lax.ppermute(value, AXES, pairs)  72.6 us
    pallas_call x1, Pallas kernels, partial_tiles(): pl.pallas_call(functools.partial(tile_kernel, counts), out_shape=jax.Shap...  11 us
    convert_element_type x3, other arithmetic, ring(): up = (upper + up.astype(jnp.float32)).astype(jnp.bfloat16)  4.33 us
    convert_element_type x3, other arithmetic, weigh(): return (piece * weights[:, at:at + piece.shape[1]]).astype(jnp.bfloat16)  4.12 us
  transfers between devices with their start and end apart: 27, of which 12 were waited for; matrix products, arithmetic and copies ran while one was open for 4% of the time, Pallas kernels for 0%

profile of v3, /device:TPU:6, one launch (start us, length us, event | category | flops | bytes accessed | tf_op | source)
XLA Modules:
  0.0 177.3 jit_solution(17381560242674359244)
XLA Ops:
  0.0 1.6 copy-done
  1.6 0.9 constant_dynamic-slice_fusion.2
  2.5 0.1 constant_dynamic-slice_fusion.1.refs_3_
  2.6 3.5 %collective-permute-start.2 = (bf16[512,1024]{1,0:T(8,128)(2,1)S(1)}, bf16[512,1024]{1,0:T(8,128)(2,1)}, u32[]{:S(2)}, u32[]{:S(2)}) collective-permute-start(bf16[512,1024]{1,0:T(8,128)(2,1)S(1)} %constant_dynamic-slice_fusion.1.refs_3_), channel_id=1, source_target_pairs={{0,16},{1,17},{2,18},{3,19},{4,20},{5,21},{6,22},{7,23},{16,32},{1... | collective-permute-start | bytes 3145736 | tf_op jit(solution)/shard_map/ppermute | solution.py:35
  6.1 2.0 %collective-permute-start.1 = (bf16[512,1024]{1,0:T(8,128)(2,1)S(1)}, bf16[512,1024]{1,0:T(8,128)(2,1)}, u32[]{:S(2)}, u32[]{:S(2)}) collective-permute-start(bf16[512,1024]{1,0:T(8,128)(2,1)S(1)} %constant_dynamic-slice_fusion.1.refs_3_), channel_id=1, source_target_pairs={{0,240},{1,241},{2,242},{3,243},{4,244},{5,245},{6,246},{7,247},{8... | collective-permute-start | bytes 3145736 | tf_op jit(solution)/shard_map/ppermute | solution.py:35
  8.1 6.6 %collective-permute-start = (bf16[512,640]{1,0:T(8,128)(2,1)}, bf16[512,640]{1,0:T(8,128)(2,1)}, u32[]{:S(2)}, u32[]{:S(2)}) collective-permute-start(bf16[512,640]{1,0:T(8,128)(2,1)} %constant_dynamic-slice_fusion.2), channel_id=1, source_target_pairs={{0,8},{1,9},{2,10},{3,11},{4,12},{5,13},{6,14},{7,15},{8,0},{9,1},... | collective-permute-start | bytes 1966088 | tf_op jit(solution)/shard_map/ppermute | solution.py:35
  14.7 0.0 collective-permute-start.6
  14.8 0.5 fusion.10
  15.4 17.6 %collective-permute-done.refs_5_ = bf16[512,640]{1,0:T(8,128)(2,1)} collective-permute-done((bf16[512,640]{1,0:T(8,128)(2,1)}, bf16[512,640]{1,0:T(8,128)(2,1)}, u32[]{:S(2)}, u32[]{:S(2)}) %collective-permute-start) | collective-permute-done | bytes 655392 | tf_op jit(solution)/shard_map/ppermute | solution.py:35
  33.0 0.0 collective-permute-done.2
  33.0 0.0 collective-permute-done.1.refs_9_
  33.0 0.0 collective-permute-start.8
  33.0 1.9 %collective-permute-start.5 = (bf16[512,1024]{1,0:T(8,128)(2,1)}, bf16[512,1024]{1,0:T(8,128)(2,1)}, u32[]{:S(2)}, u32[]{:S(2)}) collective-permute-start(bf16[512,1024]{1,0:T(8,128)(2,1)} %collective-permute-done.2), channel_id=1, source_target_pairs={{0,16},{1,17},{2,18},{3,19},{4,20},{5,21},{6,22},{7,23},{16,224},{... | collective-permute-start | bytes 3145736 | tf_op jit(solution)/shard_map/ppermute | solution.py:35
  34.9 0.6 collective-permute-start.7
  35.5 10.7 %collective-permute-start.4 = (bf16[512,640]{1,0:T(8,128)(2,1)}, bf16[512,640]{1,0:T(8,128)(2,1)S(1)}, u32[]{:S(2)}, u32[]{:S(2)}) collective-permute-start(bf16[512,640]{1,0:T(8,128)(2,1)} %collective-permute-done.refs_5_), channel_id=1, source_target_pairs={{0,240},{1,241},{2,242},{3,243},{4,244},{5,245},{6,246},{7,247},{8... | collective-permute-start | bytes 1966088 | tf_op jit(solution)/shard_map/ppermute | solution.py:35
  46.1 0.0 collective-permute-done.6.refs_4_
  46.1 1.5 collective-permute-start.9
  47.6 7.7 %collective-permute-start.3 = (bf16[528,384]{1,0:T(8,128)(2,1)S(1)}, bf16[528,384]{1,0:T(8,128)(2,1)S(1)}, u32[]{:S(2)}, u32[]{:S(2)}) collective-permute-start(bf16[528,384]{1,0:T(8,128)(2,1)S(1)} %fusion.8), channel_id=1, source_target_pairs={{0,8},{1,9},{2,10},{3,11},{4,12},{5,13},{6,14},{7,15},{8,0},{9,1},... | collective-permute-start | bytes 1216520 | tf_op jit(solution)/shard_map/ppermute | solution.py:35
  55.3 1.2 multiply_convert_fusion.refs_0_
  56.5 2.1 %multiply_convert_fusion.1.refs_1_ = bf16[512,640]{1,0:T(8,128)(2,1)} fusion(bf16[512,640]{1,0:T(8,128)(2,1)} %collective-permute-done.refs_5_, f32[640]{0:T(1024)S(1)} %slice_reduce_fusion), kind=kLoop, calls=%fused_computation.1 | loop fusion | flops 983040 | bytes 1313280 | tf_op jit(solution)/shard_map/convert_element_type | solution.py:202
  58.6 2.1 %collective-permute-done.4.refs_11_ = bf16[512,640]{1,0:T(8,128)(2,1)S(1)} collective-permute-done((bf16[512,640]{1,0:T(8,128)(2,1)}, bf16[512,640]{1,0:T(8,128)(2,1)S(1)}, u32[]{:S(2)}, u32[]{:S(2)}) %collective-permute-start.4) | collective-permute-done | bytes 655392 | tf_op jit(solution)/shard_map/ppermute | solution.py:35
  60.7 8.7 %collective-permute-done.5.refs_15_ = bf16[512,1024]{1,0:T(8,128)(2,1)} collective-permute-done((bf16[512,1024]{1,0:T(8,128)(2,1)}, bf16[512,1024]{1,0:T(8,128)(2,1)}, u32[]{:S(2)}, u32[]{:S(2)}) %collective-permute-start.5) | collective-permute-done | bytes 1048608 | tf_op jit(solution)/shard_map/ppermute | solution.py:35
  69.4 0.0 collective-permute-done.7.refs_10_
  69.4 2.9 %collective-permute-done.3.refs_6_ = bf16[528,384]{1,0:T(8,128)(2,1)S(1)} collective-permute-done((bf16[528,384]{1,0:T(8,128)(2,1)S(1)}, bf16[528,384]{1,0:T(8,128)(2,1)S(1)}, u32[]{:S(2)}, u32[]{:S(2)}) %collective-permute-start.3) | collective-permute-done | bytes 405536 | tf_op jit(solution)/shard_map/ppermute | solution.py:35
  72.3 0.0 collective-permute-done.9
  72.3 1.5 collective-permute-start.15
  73.8 1.0 collective-permute-start.10
  74.8 1.4 collective-permute-start.14
  76.3 1.4 collective-permute-start.16
  77.7 0.0 collective-permute-start.11
  77.7 0.8 multiply_convert_fusion.2.refs_2_
  78.6 4.8 %collective-permute-done.10.refs_12_ = bf16[528,384]{1,0:T(8,128)(2,1)} collective-permute-done((bf16[528,384]{1,0:T(8,128)(2,1)S(1)}, bf16[528,384]{1,0:T(8,128)(2,1)}, u32[]{:S(2)}, u32[]{:S(2)}) %collective-permute-start.10) | collective-permute-done | bytes 405536 | tf_op jit(solution)/shard_map/ppermute | solution.py:35
  83.4 1.5 collective-permute-start.17
  84.9 0.5 collective-permute-start.13
  85.4 0.0 collective-permute-done.11.refs_8_
  85.4 0.8 copy-done.6
  86.1 1.4 collective-permute-start.18
  87.6 0.8 compare_select_fusion
  88.4 0.6 reshape.54
  89.0 1.2 pad_add_fusion.table
  90.2 0.0 collective-permute-done.12.refs_13_
  90.2 0.0 collective-permute-done.14.refs_16_
  90.2 1.0 copy-done.4
  91.2 11.0 %shard_map.37 = bf16[8,4,512,128]{3,2,1,0:T(8,128)(2,1)} custom-call(s32[10]{0:T(128)} %pad_add_fusion.table, bf16[512,1024]{1,0:T(8,128)(2,1)} %multiply_convert_fusion.refs_0_, bf16[512,640]{1,0:T(8,128)(2,1)} %multiply_convert_fusion.1.refs_1_, bf16[512,384]{1,0:T(8,128)(2,1)} %multiply_convert_fusion.2.refs_2_, bf16[512,1024]{1,0:T(8,128)(2,1)} %copy-done.1, ...), custom_call_target="tpu_custom_call" | custom-call | flops 4294967296 | bytes 15728640 | tf_op jit(solution)/shard_map/pallas_call | solution.py:142
  102.2 1.1 slice_bitcast_fusion.7
  103.2 4.5 %collective-permute-start.20 = (bf16[2,512,128]{2,1,0:T(8,128)(2,1)S(1)}, bf16[2,512,128]{2,1,0:T(8,128)(2,1)S(1)}, u32[]{:S(2)}, u32[]{:S(2)}) collective-permute-start(bf16[2,512,128]{2,1,0:T(8,128)(2,1)S(1)} %get-tuple-element.79), channel_id=1, source_target_pairs={{0,1},{1,2},{2,3},{3,8},{4,5},{5,6},{6,7},{7,12},{8,9},{9,10},{10,... | collective-permute-start | bytes 786440 | tf_op jit(solution)/shard_map/ppermute | solution.py:35
  107.7 19.3 %collective-permute-start.19 = (bf16[2,512,128]{2,1,0:T(8,128)(2,1)S(1)}, bf16[2,512,128]{2,1,0:T(8,128)(2,1)S(1)}, u32[]{:S(2)}, u32[]{:S(2)}) collective-permute-start(bf16[2,512,128]{2,1,0:T(8,128)(2,1)S(1)} %get-tuple-element.80), channel_id=1, source_target_pairs={{0,11},{1,0},{2,1},{3,2},{4,15},{5,4},{6,5},{7,6},{8,3},{9,8},{10,... | collective-permute-start | bytes 786440 | tf_op jit(solution)/shard_map/ppermute | solution.py:35
  127.0 5.1 %collective-permute-done.20 = bf16[2,512,128]{2,1,0:T(8,128)(2,1)S(1)} collective-permute-done((bf16[2,512,128]{2,1,0:T(8,128)(2,1)S(1)}, bf16[2,512,128]{2,1,0:T(8,128)(2,1)S(1)}, u32[]{:S(2)}, u32[]{:S(2)}) %collective-permute-start.20) | collective-permute-done | bytes 262176 | tf_op jit(solution)/shard_map/ppermute | solution.py:35
  132.1 1.4 fusion.2
  133.4 3.1 %collective-permute-start.21 = (bf16[4,512,128]{2,1,0:T(8,128)(2,1)S(1)}, bf16[4,512,128]{2,1,0:T(8,128)(2,1)S(1)}, u32[]{:S(2)}, u32[]{:S(2)}) collective-permute-start(bf16[4,512,128]{2,1,0:T(8,128)(2,1)S(1)} %get-tuple-element.59), channel_id=1, source_target_pairs={{0,11},{1,0},{2,1},{3,2},{4,15},{5,4},{6,5},{7,6},{8,3},{9,8},{10,... | collective-permute-start | bytes 1572872 | tf_op jit(solution)/shard_map/ppermute | solution.py:35
  136.5 0.0 collective-permute-start.22
  136.5 9.1 %collective-permute-done.21 = bf16[4,512,128]{2,1,0:T(8,128)(2,1)S(1)} collective-permute-done((bf16[4,512,128]{2,1,0:T(8,128)(2,1)S(1)}, bf16[4,512,128]{2,1,0:T(8,128)(2,1)S(1)}, u32[]{:S(2)}, u32[]{:S(2)}) %collective-permute-start.21) | collective-permute-done | bytes 524320 | tf_op jit(solution)/shard_map/ppermute | solution.py:35
  145.7 3.4 %collective-permute-done.22 = bf16[4,512,128]{2,1,0:T(8,128)(2,1)S(1)} collective-permute-done((bf16[4,512,128]{2,1,0:T(8,128)(2,1)S(1)}, bf16[4,512,128]{2,1,0:T(8,128)(2,1)S(1)}, u32[]{:S(2)}, u32[]{:S(2)}) %collective-permute-start.22) | collective-permute-done | bytes 524320 | tf_op jit(solution)/shard_map/ppermute | solution.py:35
  149.1 1.5 fusion.1
  150.6 0.4 collective-permute-start.23
  150.9 1.7 collective-permute-start.24
  152.7 8.4 %collective-permute-done.23 = bf16[4,512,128]{2,1,0:T(8,128)(2,1)S(1)} collective-permute-done((bf16[4,512,128]{2,1,0:T(8,128)(2,1)S(1)}, bf16[4,512,128]{2,1,0:T(8,128)(2,1)S(1)}, u32[]{:S(2)}, u32[]{:S(2)}) %collective-permute-start.23) | collective-permute-done | bytes 524320 | tf_op jit(solution)/shard_map/ppermute | solution.py:35
  161.0 1.5 collective-permute-done.24
  162.5 1.5 fusion
  164.0 0.4 collective-permute-start.25
  164.4 1.7 collective-permute-start.26
  166.1 7.5 %collective-permute-done.25 = bf16[4,512,128]{2,1,0:T(8,128)(2,1)S(1)} collective-permute-done((bf16[4,512,128]{2,1,0:T(8,128)(2,1)S(1)}, bf16[4,512,128]{2,1,0:T(8,128)(2,1)S(1)}, u32[]{:S(2)}, u32[]{:S(2)}) %collective-permute-start.25) | collective-permute-done | bytes 524320 | tf_op jit(solution)/shard_map/ppermute | solution.py:35
  173.6 1.5 collective-permute-done.26
  175.1 2.2 %fusion.6 = f32[4,512,128]{2,1,0:T(8,128)} fusion(bf16[4,512,128]{2,1,0:T(8,128)(2,1)S(1)} %collective-permute-done.26, bf16[4,512,128]{2,1,0:T(8,128)(2,1)S(1)} %collective-permute-done.25, bf16[8,4,512,128]{3,2,1,0:T(8,128)(2,1)} %shard_map.37), kind=kLoop, calls=%fused_computation.15 | loop fusion | flops 1310720 | bytes 2621440 | tf_op jit(solution)/shard_map/add | solution.py:179
  (30 shorter events, 0.2 us)
Async XLA Ops:
  0.0 1.6 copy-start
  1.6 13.2 %copy-start.8 = (s32[1,4]{1,0:T(1,128)S(1)}, s32[1,4]{1,0:T(1,128)}, u32[]{:S(2)}) copy-start(s32[1,4]{1,0:T(1,128)} %param.5) | copy-start | bytes 52
  2.5 45.1 %copy-start.7 = (f32[2048]{0:T(1024)S(1)}, f32[2048]{0:T(1024)}, u32[]{:S(2)}) copy-start(f32[2048]{0:T(1024)} %param.4) | copy-start | bytes 24580
  2.6 56.0 %copy-start.1 = (bf16[512,1024]{1,0:T(8,128)(2,1)}, bf16[512,1024]{1,0:T(8,128)(2,1)S(1)}, u32[]{:S(2)}) copy-start(bf16[512,1024]{1,0:T(8,128)(2,1)S(1)} %constant_dynamic-slice_fusion.1.refs_3_) | copy-start | bytes 3145732
  2.6 30.3 %collective-permute-start.2 = (bf16[512,1024]{1,0:T(8,128)(2,1)S(1)}, bf16[512,1024]{1,0:T(8,128)(2,1)}, u32[]{:S(2)}, u32[]{:S(2)}) collective-permute-start(bf16[512,1024]{1,0:T(8,128)(2,1)S(1)} %constant_dynamic-slice_fusion.1.refs_3_), channel_id=1, source_target_pairs={{0,16},{1,17},{2,18},{3,19},{4,20},{5,21},{6,22},{7,23},{16,32},{1... | collective-permute-start | bytes 3145736 | tf_op jit(solution)/shard_map/ppermute | solution.py:35
  6.1 26.9 %collective-permute-start.1 = (bf16[512,1024]{1,0:T(8,128)(2,1)S(1)}, bf16[512,1024]{1,0:T(8,128)(2,1)}, u32[]{:S(2)}, u32[]{:S(2)}) collective-permute-start(bf16[512,1024]{1,0:T(8,128)(2,1)S(1)} %constant_dynamic-slice_fusion.1.refs_3_), channel_id=1, source_target_pairs={{0,240},{1,241},{2,242},{3,243},{4,244},{5,245},{6,246},{7,247},{8... | collective-permute-start | bytes 3145736 | tf_op jit(solution)/shard_map/ppermute | solution.py:35
  8.1 24.8 %collective-permute-start = (bf16[512,640]{1,0:T(8,128)(2,1)}, bf16[512,640]{1,0:T(8,128)(2,1)}, u32[]{:S(2)}, u32[]{:S(2)}) collective-permute-start(bf16[512,640]{1,0:T(8,128)(2,1)} %constant_dynamic-slice_fusion.2), channel_id=1, source_target_pairs={{0,8},{1,9},{2,10},{3,11},{4,12},{5,13},{6,14},{7,15},{8,0},{9,1},... | collective-permute-start | bytes 1966088 | tf_op jit(solution)/shard_map/ppermute | solution.py:35
  14.7 31.4 %collective-permute-start.6 = (bf16[512,1024]{1,0:T(8,128)(2,1)S(1)}, bf16[512,1024]{1,0:T(8,128)(2,1)}, u32[]{:S(2)}, u32[]{:S(2)}) collective-permute-start(bf16[512,1024]{1,0:T(8,128)(2,1)S(1)} %constant_dynamic-slice_fusion.1.refs_3_), channel_id=1, source_target_pairs={{0,4},{1,5},{2,6},{3,7},{4,0},{5,1},{6,2},{7,3},{8,12},{9,13},{10,... | collective-permute-start | bytes 3145736 | tf_op jit(solution)/shard_map/ppermute | solution.py:35
  33.0 14.7 %collective-permute-start.8 = (bf16[512,640]{1,0:T(8,128)(2,1)}, bf16[512,640]{1,0:T(8,128)(2,1)}, u32[]{:S(2)}, u32[]{:S(2)}) collective-permute-start(bf16[512,640]{1,0:T(8,128)(2,1)} %collective-permute-done.refs_5_), channel_id=1, source_target_pairs={{0,4},{1,5},{2,6},{3,7},{4,0},{5,1},{6,2},{7,3},{8,12},{9,13},{10,... | collective-permute-start | bytes 1966088 | tf_op jit(solution)/shard_map/ppermute | solution.py:35
  33.0 36.4 %collective-permute-start.5 = (bf16[512,1024]{1,0:T(8,128)(2,1)}, bf16[512,1024]{1,0:T(8,128)(2,1)}, u32[]{:S(2)}, u32[]{:S(2)}) collective-permute-start(bf16[512,1024]{1,0:T(8,128)(2,1)} %collective-permute-done.2), channel_id=1, source_target_pairs={{0,16},{1,17},{2,18},{3,19},{4,20},{5,21},{6,22},{7,23},{16,224},{... | collective-permute-start | bytes 3145736 | tf_op jit(solution)/shard_map/ppermute | solution.py:35
  34.9 34.5 %collective-permute-start.7 = (bf16[512,1024]{1,0:T(8,128)(2,1)}, bf16[512,1024]{1,0:T(8,128)(2,1)S(1)}, u32[]{:S(2)}, u32[]{:S(2)}) collective-permute-start(bf16[512,1024]{1,0:T(8,128)(2,1)} %collective-permute-done.1.refs_9_), channel_id=1, source_target_pairs={{0,4},{1,5},{2,6},{3,7},{4,0},{5,1},{6,2},{7,3},{8,12},{9,13},{10,... | collective-permute-start | bytes 3145736 | tf_op jit(solution)/shard_map/ppermute | solution.py:35
  35.5 25.2 %collective-permute-start.4 = (bf16[512,640]{1,0:T(8,128)(2,1)}, bf16[512,640]{1,0:T(8,128)(2,1)S(1)}, u32[]{:S(2)}, u32[]{:S(2)}) collective-permute-start(bf16[512,640]{1,0:T(8,128)(2,1)} %collective-permute-done.refs_5_), channel_id=1, source_target_pairs={{0,240},{1,241},{2,242},{3,243},{4,244},{5,245},{6,246},{7,247},{8... | collective-permute-start | bytes 1966088 | tf_op jit(solution)/shard_map/ppermute | solution.py:35
  46.1 26.2 %collective-permute-start.9 = (bf16[512,640]{1,0:T(8,128)(2,1)}, bf16[512,640]{1,0:T(8,128)(2,1)}, u32[]{:S(2)}, u32[]{:S(2)}) collective-permute-start(bf16[512,640]{1,0:T(8,128)(2,1)} %collective-permute-done.refs_5_), channel_id=1, source_target_pairs={{8,24},{9,25},{10,26},{11,27},{12,28},{13,29},{14,30},{15,31},{24,... | collective-permute-start | bytes 1966088 | tf_op jit(solution)/shard_map/ppermute | solution.py:35
  47.6 24.7 %collective-permute-start.3 = (bf16[528,384]{1,0:T(8,128)(2,1)S(1)}, bf16[528,384]{1,0:T(8,128)(2,1)S(1)}, u32[]{:S(2)}, u32[]{:S(2)}) collective-permute-start(bf16[528,384]{1,0:T(8,128)(2,1)S(1)} %fusion.8), channel_id=1, source_target_pairs={{0,8},{1,9},{2,10},{3,11},{4,12},{5,13},{6,14},{7,15},{8,0},{9,1},... | collective-permute-start | bytes 1216520 | tf_op jit(solution)/shard_map/ppermute | solution.py:35
  60.7 13.1 %copy-start.5 = (bf16[512,640]{1,0:T(8,128)(2,1)}, bf16[512,640]{1,0:T(8,128)(2,1)S(1)}, u32[]{:S(2)}) copy-start(bf16[512,640]{1,0:T(8,128)(2,1)S(1)} %collective-permute-done.4.refs_11_) | copy-start | bytes 1966084
  69.4 2.9 %copy-start.3 = (bf16[512,1024]{1,0:T(8,128)(2,1)}, bf16[512,1024]{1,0:T(8,128)(2,1)S(1)}, u32[]{:S(2)}) copy-start(bf16[512,1024]{1,0:T(8,128)(2,1)S(1)} %collective-permute-done.7.refs_10_) | copy-start | bytes 3145732
  72.3 17.9 %copy-start.2 = (bf16[528,384]{1,0:T(8,128)(2,1)}, bf16[528,384]{1,0:T(8,128)(2,1)S(1)}, u32[]{:S(2)}) copy-start(bf16[528,384]{1,0:T(8,128)(2,1)S(1)} %collective-permute-done.3.refs_6_) | copy-start | bytes 1216516
  72.3 11.0 %collective-permute-start.15 = (bf16[512,640]{1,0:T(8,128)(2,1)}, bf16[512,640]{1,0:T(8,128)(2,1)}, u32[]{:S(2)}, u32[]{:S(2)}) collective-permute-start(bf16[512,640]{1,0:T(8,128)(2,1)} %collective-permute-done.9), channel_id=1, source_target_pairs={{8,24},{9,25},{10,26},{11,27},{12,28},{13,29},{14,30},{15,31},{24,... | collective-permute-start | bytes 1966088 | tf_op jit(solution)/shard_map/ppermute | solution.py:35
  73.8 9.5 %collective-permute-start.10 = (bf16[528,384]{1,0:T(8,128)(2,1)S(1)}, bf16[528,384]{1,0:T(8,128)(2,1)}, u32[]{:S(2)}, u32[]{:S(2)}) collective-permute-start(bf16[528,384]{1,0:T(8,128)(2,1)S(1)} %collective-permute-done.3.refs_6_), channel_id=1, source_target_pairs={{0,240},{1,241},{2,242},{3,243},{4,244},{5,245},{6,246},{7,247},{8... | collective-permute-start | bytes 1216520 | tf_op jit(solution)/shard_map/ppermute | solution.py:35
  74.8 15.3 %collective-permute-start.14 = (bf16[512,1024]{1,0:T(8,128)(2,1)}, bf16[512,1024]{1,0:T(8,128)(2,1)S(1)}, u32[]{:S(2)}, u32[]{:S(2)}) collective-permute-start(bf16[512,1024]{1,0:T(8,128)(2,1)} %collective-permute-done.5.refs_15_), channel_id=1, source_target_pairs={{0,4},{1,5},{2,6},{3,7},{16,20},{17,21},{18,22},{19,23},{32,36},{3... | collective-permute-start | bytes 3145736 | tf_op jit(solution)/shard_map/ppermute | solution.py:35
  76.3 8.6 %collective-permute-start.16 = (bf16[528,384]{1,0:T(8,128)(2,1)S(1)}, bf16[528,384]{1,0:T(8,128)(2,1)}, u32[]{:S(2)}, u32[]{:S(2)}) collective-permute-start(bf16[528,384]{1,0:T(8,128)(2,1)S(1)} %collective-permute-done.3.refs_6_), channel_id=1, source_target_pairs={{8,232},{9,233},{10,234},{11,235},{12,236},{13,237},{14,238},{15,2... | collective-permute-start | bytes 1216520 | tf_op jit(solution)/shard_map/ppermute | solution.py:35
  77.7 7.7 %collective-permute-start.11 = (bf16[528,384]{1,0:T(8,128)(2,1)S(1)}, bf16[528,384]{1,0:T(8,128)(2,1)S(1)}, u32[]{:S(2)}, u32[]{:S(2)}) collective-permute-start(bf16[528,384]{1,0:T(8,128)(2,1)S(1)} %collective-permute-done.3.refs_6_), channel_id=1, source_target_pairs={{0,4},{1,5},{2,6},{3,7},{4,0},{5,1},{6,2},{7,3},{8,12},{9,13},{10,... | collective-permute-start | bytes 1216520 | tf_op jit(solution)/shard_map/ppermute | solution.py:35
  83.4 6.8 %collective-permute-start.12 = (bf16[512,640]{1,0:T(8,128)(2,1)}, bf16[512,640]{1,0:T(8,128)(2,1)}, u32[]{:S(2)}, u32[]{:S(2)}) collective-permute-start(bf16[512,640]{1,0:T(8,128)(2,1)} %copy-done.5), channel_id=1, source_target_pairs={{0,4},{1,5},{2,6},{3,7},{4,0},{5,1},{6,2},{7,3},{8,12},{9,13},{10,... | collective-permute-start | bytes 1966088 | tf_op jit(solution)/shard_map/ppermute | solution.py:35
  83.4 6.8 %collective-permute-start.17 = (bf16[512,640]{1,0:T(8,128)(2,1)}, bf16[512,640]{1,0:T(8,128)(2,1)}, u32[]{:S(2)}, u32[]{:S(2)}) collective-permute-start(bf16[512,640]{1,0:T(8,128)(2,1)} %collective-permute-done.15.refs_17_), channel_id=1, source_target_pairs={{8,12},{9,13},{10,14},{11,15},{24,28},{25,29},{26,30},{27,31},{40,... | collective-permute-start | bytes 1966088 | tf_op jit(solution)/shard_map/ppermute | solution.py:35
  84.9 5.3 %collective-permute-start.13 = (bf16[528,384]{1,0:T(8,128)(2,1)}, bf16[528,384]{1,0:T(8,128)(2,1)}, u32[]{:S(2)}, u32[]{:S(2)}) collective-permute-start(bf16[528,384]{1,0:T(8,128)(2,1)} %collective-permute-done.10.refs_12_), channel_id=1, source_target_pairs={{0,4},{1,5},{2,6},{3,7},{4,0},{5,1},{6,2},{7,3},{8,12},{9,13},{10,... | collective-permute-start | bytes 1216520 | tf_op jit(solution)/shard_map/ppermute | solution.py:35
  85.4 0.8 copy-start.6
  86.1 4.0 %collective-permute-start.18 = (bf16[528,384]{1,0:T(8,128)(2,1)}, bf16[528,384]{1,0:T(8,128)(2,1)}, u32[]{:S(2)}, u32[]{:S(2)}) collective-permute-start(bf16[528,384]{1,0:T(8,128)(2,1)} %collective-permute-done.16.refs_18_), channel_id=1, source_target_pairs={{8,12},{9,13},{10,14},{11,15},{24,28},{25,29},{26,30},{27,31},{40,... | collective-permute-start | bytes 1216520 | tf_op jit(solution)/shard_map/ppermute | solution.py:35
  90.2 1.0 copy-start.4
  103.2 28.8 %collective-permute-start.20 = (bf16[2,512,128]{2,1,0:T(8,128)(2,1)S(1)}, bf16[2,512,128]{2,1,0:T(8,128)(2,1)S(1)}, u32[]{:S(2)}, u32[]{:S(2)}) collective-permute-start(bf16[2,512,128]{2,1,0:T(8,128)(2,1)S(1)} %get-tuple-element.79), channel_id=1, source_target_pairs={{0,1},{1,2},{2,3},{3,8},{4,5},{5,6},{6,7},{7,12},{8,9},{9,10},{10,... | collective-permute-start | bytes 786440 | tf_op jit(solution)/shard_map/ppermute | solution.py:35
  107.7 24.4 %collective-permute-start.19 = (bf16[2,512,128]{2,1,0:T(8,128)(2,1)S(1)}, bf16[2,512,128]{2,1,0:T(8,128)(2,1)S(1)}, u32[]{:S(2)}, u32[]{:S(2)}) collective-permute-start(bf16[2,512,128]{2,1,0:T(8,128)(2,1)S(1)} %get-tuple-element.80), channel_id=1, source_target_pairs={{0,11},{1,0},{2,1},{3,2},{4,15},{5,4},{6,5},{7,6},{8,3},{9,8},{10,... | collective-permute-start | bytes 786440 | tf_op jit(solution)/shard_map/ppermute | solution.py:35
  133.4 12.2 %collective-permute-start.21 = (bf16[4,512,128]{2,1,0:T(8,128)(2,1)S(1)}, bf16[4,512,128]{2,1,0:T(8,128)(2,1)S(1)}, u32[]{:S(2)}, u32[]{:S(2)}) collective-permute-start(bf16[4,512,128]{2,1,0:T(8,128)(2,1)S(1)} %get-tuple-element.59), channel_id=1, source_target_pairs={{0,11},{1,0},{2,1},{3,2},{4,15},{5,4},{6,5},{7,6},{8,3},{9,8},{10,... | collective-permute-start | bytes 1572872 | tf_op jit(solution)/shard_map/ppermute | solution.py:35
  136.5 12.5 %collective-permute-start.22 = (bf16[4,512,128]{2,1,0:T(8,128)(2,1)S(1)}, bf16[4,512,128]{2,1,0:T(8,128)(2,1)S(1)}, u32[]{:S(2)}, u32[]{:S(2)}) collective-permute-start(bf16[4,512,128]{2,1,0:T(8,128)(2,1)S(1)} %get-tuple-element.60), channel_id=1, source_target_pairs={{0,1},{1,2},{2,3},{3,8},{4,5},{5,6},{6,7},{7,12},{8,9},{9,10},{10,... | collective-permute-start | bytes 1572872 | tf_op jit(solution)/shard_map/ppermute | solution.py:35
  150.6 10.5 %collective-permute-start.23 = (bf16[4,512,128]{2,1,0:T(8,128)(2,1)S(1)}, bf16[4,512,128]{2,1,0:T(8,128)(2,1)S(1)}, u32[]{:S(2)}, u32[]{:S(2)}) collective-permute-start(bf16[4,512,128]{2,1,0:T(8,128)(2,1)S(1)} %get-tuple-element.63), channel_id=1, source_target_pairs={{0,11},{1,0},{2,1},{3,2},{4,15},{5,4},{6,5},{7,6},{8,3},{9,8},{10,... | collective-permute-start | bytes 1572872 | tf_op jit(solution)/shard_map/ppermute | solution.py:35
  150.9 11.6 %collective-permute-start.24 = (bf16[4,512,128]{2,1,0:T(8,128)(2,1)S(1)}, bf16[4,512,128]{2,1,0:T(8,128)(2,1)S(1)}, u32[]{:S(2)}, u32[]{:S(2)}) collective-permute-start(bf16[4,512,128]{2,1,0:T(8,128)(2,1)S(1)} %get-tuple-element.64), channel_id=1, source_target_pairs={{0,1},{1,2},{2,3},{3,8},{4,5},{5,6},{6,7},{7,12},{8,9},{9,10},{10,... | collective-permute-start | bytes 1572872 | tf_op jit(solution)/shard_map/ppermute | solution.py:35
  164.0 9.6 %collective-permute-start.25 = (bf16[4,512,128]{2,1,0:T(8,128)(2,1)S(1)}, bf16[4,512,128]{2,1,0:T(8,128)(2,1)S(1)}, u32[]{:S(2)}, u32[]{:S(2)}) collective-permute-start(bf16[4,512,128]{2,1,0:T(8,128)(2,1)S(1)} %get-tuple-element.67), channel_id=1, source_target_pairs={{0,11},{1,0},{2,1},{3,2},{4,15},{5,4},{6,5},{7,6},{8,3},{9,8},{10,... | collective-permute-start | bytes 1572872 | tf_op jit(solution)/shard_map/ppermute | solution.py:35
  164.4 10.7 %collective-permute-start.26 = (bf16[4,512,128]{2,1,0:T(8,128)(2,1)S(1)}, bf16[4,512,128]{2,1,0:T(8,128)(2,1)S(1)}, u32[]{:S(2)}, u32[]{:S(2)}) collective-permute-start(bf16[4,512,128]{2,1,0:T(8,128)(2,1)S(1)} %get-tuple-element.68), channel_id=1, source_target_pairs={{0,1},{1,2},{2,3},{3,8},{4,5},{5,6},{6,7},{7,12},{8,9},{9,10},{10,... | collective-permute-start | bytes 1572872 | tf_op jit(solution)/shard_map/ppermute | solution.py:35

commit v4 on v3

--- a/solution.py
+++ b/solution.py
@@ -10,7 +10,7 @@
 SLOTS = 4
 TB = 512
 WIDE = 1024
-WIDTHS = (640, 384)
+WIDTHS = (512, 512)
 DEPTH = 4
 AXES = ("trans", "pw")
 

time: 178 us -> 192 us (1.079)
  the two profiles are of different devices: /device:TPU:6 before, /device:TPU:16 now
where the time goes in v4:
time: 192 us
  waiting for transfers between devices  94.4 us (49%)
  starting transfers between devices  69 us (36%)
  Pallas kernels  11 us (6%)
  other arithmetic  10.3 us (5%)
  local copies, waits for them, and re-layouts  7.09 us (4%)
    ppermute x27, waiting for transfers between devices, send(): return lax.ppermute(value, AXES, pairs)  94.4 us
    ppermute x27, starting transfers between devices, send(): return lax.ppermute(value, AXES, pairs)  69 us
    pallas_call x1, Pallas kernels, partial_tiles(): pl.pallas_call(functools.partial(tile_kernel, counts), out_shape=jax.Shap...  11 us
    unnamed x32, local copies, waits for them, and re-layouts  4.39 us
    convert_element_type x3, other arithmetic, ring(): up = (upper + up.astype(jnp.float32)).astype(jnp.bfloat16)  4.33 us
  transfers between devices with their start and end apart: 27, of which 14 were waited for; matrix products, arithmetic and copies ran while one was open for 2% of the time, Pallas kernels for 0%

profile of v4, /device:TPU:16, one launch (start us, length us, event | category | flops | bytes accessed | tf_op | source)
XLA Modules:
  0.0 191.9 jit_solution(329079658776264428)
XLA Ops:
  0.0 1.4 constant_dynamic-slice_fusion.1.refs_3_
  1.4 0.5 copy-done.3
  1.9 0.1 constant_dynamic-slice_fusion
  2.0 3.2 %collective-permute-start.2 = (bf16[512,1024]{1,0:T(8,128)(2,1)S(1)}, bf16[512,1024]{1,0:T(8,128)(2,1)S(1)}, u32[]{:S(2)}, u32[]{:S(2)}) collective-permute-start(bf16[512,1024]{1,0:T(8,128)(2,1)S(1)} %constant_dynamic-slice_fusion.1.refs_3_), channel_id=1, source_target_pairs={{0,16},{1,17},{2,18},{3,19},{4,20},{5,21},{6,22},{7,23},{16,32},{1... | collective-permute-start | bytes 3145736 | tf_op jit(solution)/shard_map/ppermute | solution.py:35
  5.2 0.8 collective-permute-start.1
  6.0 4.4 %collective-permute-start = (bf16[512,512]{1,0:T(8,128)(2,1)S(1)}, bf16[512,512]{1,0:T(8,128)(2,1)S(1)}, u32[]{:S(2)}, u32[]{:S(2)}) collective-permute-start(bf16[512,512]{1,0:T(8,128)(2,1)S(1)} %get-tuple-element.38), channel_id=1, source_target_pairs={{0,8},{1,9},{2,10},{3,11},{4,12},{5,13},{6,14},{7,15},{8,0},{9,1},... | collective-permute-start | bytes 1572872 | tf_op jit(solution)/shard_map/ppermute | solution.py:35
  10.5 0.0 collective-permute-start.6
  10.5 14.8 %collective-permute-done.refs_5_ = bf16[512,512]{1,0:T(8,128)(2,1)S(1)} collective-permute-done((bf16[512,512]{1,0:T(8,128)(2,1)S(1)}, bf16[512,512]{1,0:T(8,128)(2,1)S(1)}, u32[]{:S(2)}, u32[]{:S(2)}) %collective-permute-start) | collective-permute-done | bytes 524320 | tf_op jit(solution)/shard_map/ppermute | solution.py:35
  25.3 3.5 %collective-permute-done.2 = bf16[512,1024]{1,0:T(8,128)(2,1)S(1)} collective-permute-done((bf16[512,1024]{1,0:T(8,128)(2,1)S(1)}, bf16[512,1024]{1,0:T(8,128)(2,1)S(1)}, u32[]{:S(2)}, u32[]{:S(2)}) %collective-permute-start.2) | collective-permute-done | bytes 1048608 | tf_op jit(solution)/shard_map/ppermute | solution.py:35
  28.8 1.1 collective-permute-done.1.refs_9_
  29.9 0.0 collective-permute-start.8
  29.9 7.7 %collective-permute-start.5 = (bf16[512,1024]{1,0:T(8,128)(2,1)S(1)}, bf16[512,1024]{1,0:T(8,128)(2,1)}, u32[]{:S(2)}, u32[]{:S(2)}) collective-permute-start(bf16[512,1024]{1,0:T(8,128)(2,1)S(1)} %collective-permute-done.2), channel_id=1, source_target_pairs={{0,16},{1,17},{2,18},{3,19},{4,20},{5,21},{6,22},{7,23},{16,224},{... | collective-permute-start | bytes 3145736 | tf_op jit(solution)/shard_map/ppermute | solution.py:35
  37.6 0.3 collective-permute-start.7
  38.0 0.0 collective-permute-start.3
  38.0 0.7 collective-permute-start.9
  38.7 0.0 collective-permute-done.8.refs_7_
  38.7 0.3 copy-done.5
  39.0 0.8 copy-done.11
  39.7 0.0 collective-permute-start.4
  39.7 1.2 multiply_convert_fusion.refs_0_
  41.0 0.9 multiply_convert_fusion.2.refs_1_
  41.9 13.6 %collective-permute-done.4.refs_11_ = bf16[512,512]{1,0:T(8,128)(2,1)S(1)} collective-permute-done((bf16[512,512]{1,0:T(8,128)(2,1)S(1)}, bf16[512,512]{1,0:T(8,128)(2,1)S(1)}, u32[]{:S(2)}, u32[]{:S(2)}) %collective-permute-start.4) | collective-permute-done | bytes 524320 | tf_op jit(solution)/shard_map/ppermute | solution.py:35
  55.5 5.2 %collective-permute-done.5.refs_15_ = bf16[512,1024]{1,0:T(8,128)(2,1)} collective-permute-done((bf16[512,1024]{1,0:T(8,128)(2,1)S(1)}, bf16[512,1024]{1,0:T(8,128)(2,1)}, u32[]{:S(2)}, u32[]{:S(2)}) %collective-permute-start.5) | collective-permute-done | bytes 1048608 | tf_op jit(solution)/shard_map/ppermute | solution.py:35
  60.7 7.2 %collective-permute-done.3.refs_6_ = bf16[528,512]{1,0:T(8,128)(2,1)S(1)} collective-permute-done((bf16[528,512]{1,0:T(8,128)(2,1)S(1)}, bf16[528,512]{1,0:T(8,128)(2,1)S(1)}, u32[]{:S(2)}, u32[]{:S(2)}) %collective-permute-start.3) | collective-permute-done | bytes 540704 | tf_op jit(solution)/shard_map/ppermute | solution.py:35
  67.9 1.5 collective-permute-start.16
  69.4 1.4 collective-permute-start.15
  70.9 1.3 collective-permute-start.14
  72.2 0.1 collective-permute-start.12
  72.3 0.9 multiply_convert_fusion.1.refs_2_
  73.2 5.5 %collective-permute-done.10.refs_12_ = bf16[528,512]{1,0:T(8,128)(2,1)} collective-permute-done((bf16[528,512]{1,0:T(8,128)(2,1)S(1)}, bf16[528,512]{1,0:T(8,128)(2,1)}, u32[]{:S(2)}, u32[]{:S(2)}) %collective-permute-start.10) | collective-permute-done | bytes 540704 | tf_op jit(solution)/shard_map/ppermute | solution.py:35
  78.7 0.0 collective-permute-start.11
  78.7 0.7 collective-permute-start.18
  79.4 0.0 collective-permute-done.15.refs_17_
  79.5 0.6 collective-permute-start.13
  80.0 0.8 copy-done.13
  80.8 1.5 collective-permute-start.17
  82.3 0.1 compare_select_fusion
  82.4 0.1 reshape.54
  82.5 0.6 pad_add_fusion.table
  83.2 0.8 copy-done.8
  84.0 0.3 copy-done.7
  84.3 0.2 copy-done.9
  84.4 0.8 copy-done.10
  85.2 11.0 %shard_map.37 = bf16[8,4,512,128]{3,2,1,0:T(8,128)(2,1)} custom-call(s32[10]{0:T(128)} %pad_add_fusion.table, bf16[512,1024]{1,0:T(8,128)(2,1)} %multiply_convert_fusion.refs_0_, bf16[512,512]{1,0:T(8,128)(2,1)} %multiply_convert_fusion.2.refs_1_, bf16[512,512]{1,0:T(8,128)(2,1)} %multiply_convert_fusion.1.refs_2_, bf16[512,1024]{1,0:T(8,128)(2,1)} %copy-done, ...), custom_call_target="tpu_custom_call" | custom-call | flops 4294967296 | bytes 15728640 | tf_op jit(solution)/shard_map/pallas_call | solution.py:142
  96.2 1.1 slice_bitcast_fusion.7
  97.3 0.1 collective-permute-start.20
  97.3 36.7 %collective-permute-start.19 = (bf16[2,512,128]{2,1,0:T(8,128)(2,1)S(1)}, bf16[2,512,128]{2,1,0:T(8,128)(2,1)S(1)}, u32[]{:S(2)}, u32[]{:S(2)}) collective-permute-start(bf16[2,512,128]{2,1,0:T(8,128)(2,1)S(1)} %get-tuple-element.80), channel_id=1, source_target_pairs={{0,11},{1,0},{2,1},{3,2},{4,15},{5,4},{6,5},{7,6},{8,3},{9,8},{10,... | collective-permute-start | bytes 786440 | tf_op jit(solution)/shard_map/ppermute | solution.py:35
  134.1 6.5 %collective-permute-done.20 = bf16[2,512,128]{2,1,0:T(8,128)(2,1)S(1)} collective-permute-done((bf16[2,512,128]{2,1,0:T(8,128)(2,1)S(1)}, bf16[2,512,128]{2,1,0:T(8,128)(2,1)S(1)}, u32[]{:S(2)}, u32[]{:S(2)}) %collective-permute-start.20) | collective-permute-done | bytes 262176 | tf_op jit(solution)/shard_map/ppermute | solution.py:35
  140.6 1.4 fusion.3
  141.9 3.7 %collective-permute-start.21 = (bf16[4,512,128]{2,1,0:T(8,128)(2,1)S(1)}, bf16[4,512,128]{2,1,0:T(8,128)(2,1)S(1)}, u32[]{:S(2)}, u32[]{:S(2)}) collective-permute-start(bf16[4,512,128]{2,1,0:T(8,128)(2,1)S(1)} %get-tuple-element.59), channel_id=1, source_target_pairs={{0,11},{1,0},{2,1},{3,2},{4,15},{5,4},{6,5},{7,6},{8,3},{9,8},{10,... | collective-permute-start | bytes 1572872 | tf_op jit(solution)/shard_map/ppermute | solution.py:35
  145.6 0.0 collective-permute-start.22
  145.6 11.0 %collective-permute-done.21 = bf16[4,512,128]{2,1,0:T(8,128)(2,1)S(1)} collective-permute-done((bf16[4,512,128]{2,1,0:T(8,128)(2,1)S(1)}, bf16[4,512,128]{2,1,0:T(8,128)(2,1)S(1)}, u32[]{:S(2)}, u32[]{:S(2)}) %collective-permute-start.21) | collective-permute-done | bytes 524320 | tf_op jit(solution)/shard_map/ppermute | solution.py:35
  156.6 3.4 %collective-permute-done.22 = bf16[4,512,128]{2,1,0:T(8,128)(2,1)S(1)} collective-permute-done((bf16[4,512,128]{2,1,0:T(8,128)(2,1)S(1)}, bf16[4,512,128]{2,1,0:T(8,128)(2,1)S(1)}, u32[]{:S(2)}, u32[]{:S(2)}) %collective-permute-start.22) | collective-permute-done | bytes 524320 | tf_op jit(solution)/shard_map/ppermute | solution.py:35
  160.0 1.5 fusion.2
  161.5 0.4 collective-permute-start.23
  161.9 1.7 collective-permute-start.24
  163.6 10.2 %collective-permute-done.23 = bf16[4,512,128]{2,1,0:T(8,128)(2,1)S(1)} collective-permute-done((bf16[4,512,128]{2,1,0:T(8,128)(2,1)S(1)}, bf16[4,512,128]{2,1,0:T(8,128)(2,1)S(1)}, u32[]{:S(2)}, u32[]{:S(2)}) %collective-permute-start.23) | collective-permute-done | bytes 524320 | tf_op jit(solution)/shard_map/ppermute | solution.py:35
  173.8 1.5 collective-permute-done.24
  175.3 1.5 fusion.1
  176.8 0.4 collective-permute-start.25
  177.2 1.7 collective-permute-start.26
  178.9 9.3 %collective-permute-done.25 = bf16[4,512,128]{2,1,0:T(8,128)(2,1)S(1)} collective-permute-done((bf16[4,512,128]{2,1,0:T(8,128)(2,1)S(1)}, bf16[4,512,128]{2,1,0:T(8,128)(2,1)S(1)}, u32[]{:S(2)}, u32[]{:S(2)}) %collective-permute-start.25) | collective-permute-done | bytes 524320 | tf_op jit(solution)/shard_map/ppermute | solution.py:35
  188.3 1.5 collective-permute-done.26
  189.7 2.2 %fusion.7 = f32[4,512,128]{2,1,0:T(8,128)} fusion(bf16[4,512,128]{2,1,0:T(8,128)(2,1)S(1)} %collective-permute-done.26, bf16[4,512,128]{2,1,0:T(8,128)(2,1)S(1)} %collective-permute-done.25, bf16[8,4,512,128]{3,2,1,0:T(8,128)(2,1)} %shard_map.37), kind=kLoop, calls=%fused_computation.16 | loop fusion | flops 1310720 | bytes 2621440 | tf_op jit(solution)/shard_map/add | solution.py:179
  (42 shorter events, 0.1 us)
Async XLA Ops:
  0.0 1.9 copy-start.3
  0.0 10.5 %copy-start.15 = (s32[1,4]{1,0:T(1,128)S(1)}, s32[1,4]{1,0:T(1,128)}, u32[]{:S(2)}) copy-start(s32[1,4]{1,0:T(1,128)} %param.5) | copy-start | bytes 52
  1.9 39.1 %copy-start = (bf16[512,1024]{1,0:T(8,128)(2,1)}, bf16[512,1024]{1,0:T(8,128)(2,1)S(1)}, u32[]{:S(2)}) copy-start(bf16[512,1024]{1,0:T(8,128)(2,1)S(1)} %constant_dynamic-slice_fusion.1.refs_3_) | copy-start | bytes 3145732
  1.9 36.0 %copy-start.14 = (f32[2048]{0:T(1024)S(1)}, f32[2048]{0:T(1024)}, u32[]{:S(2)}) copy-start(f32[2048]{0:T(1024)} %param.4) | copy-start | bytes 24580
  2.0 26.8 %collective-permute-start.2 = (bf16[512,1024]{1,0:T(8,128)(2,1)S(1)}, bf16[512,1024]{1,0:T(8,128)(2,1)S(1)}, u32[]{:S(2)}, u32[]{:S(2)}) collective-permute-start(bf16[512,1024]{1,0:T(8,128)(2,1)S(1)} %constant_dynamic-slice_fusion.1.refs_3_), channel_id=1, source_target_pairs={{0,16},{1,17},{2,18},{3,19},{4,20},{5,21},{6,22},{7,23},{16,32},{1... | collective-permute-start | bytes 3145736 | tf_op jit(solution)/shard_map/ppermute | solution.py:35
  5.2 24.7 %collective-permute-start.1 = (bf16[512,1024]{1,0:T(8,128)(2,1)S(1)}, bf16[512,1024]{1,0:T(8,128)(2,1)S(1)}, u32[]{:S(2)}, u32[]{:S(2)}) collective-permute-start(bf16[512,1024]{1,0:T(8,128)(2,1)S(1)} %constant_dynamic-slice_fusion.1.refs_3_), channel_id=1, source_target_pairs={{0,240},{1,241},{2,242},{3,243},{4,244},{5,245},{6,246},{7,247},{8... | collective-permute-start | bytes 3145736 | tf_op jit(solution)/shard_map/ppermute | solution.py:35
  6.0 19.3 %collective-permute-start = (bf16[512,512]{1,0:T(8,128)(2,1)S(1)}, bf16[512,512]{1,0:T(8,128)(2,1)S(1)}, u32[]{:S(2)}, u32[]{:S(2)}) collective-permute-start(bf16[512,512]{1,0:T(8,128)(2,1)S(1)} %get-tuple-element.38), channel_id=1, source_target_pairs={{0,8},{1,9},{2,10},{3,11},{4,12},{5,13},{6,14},{7,15},{8,0},{9,1},... | collective-permute-start | bytes 1572872 | tf_op jit(solution)/shard_map/ppermute | solution.py:35
  10.5 27.5 %collective-permute-start.6 = (bf16[512,1024]{1,0:T(8,128)(2,1)S(1)}, bf16[512,1024]{1,0:T(8,128)(2,1)S(1)}, u32[]{:S(2)}, u32[]{:S(2)}) collective-permute-start(bf16[512,1024]{1,0:T(8,128)(2,1)S(1)} %constant_dynamic-slice_fusion.1.refs_3_), channel_id=1, source_target_pairs={{0,4},{1,5},{2,6},{3,7},{4,0},{5,1},{6,2},{7,3},{8,12},{9,13},{10,... | collective-permute-start | bytes 3145736 | tf_op jit(solution)/shard_map/ppermute | solution.py:35
  25.3 47.9 %copy-start.2 = (bf16[512,512]{1,0:T(8,128)(2,1)}, bf16[512,512]{1,0:T(8,128)(2,1)S(1)}, u32[]{:S(2)}) copy-start(bf16[512,512]{1,0:T(8,128)(2,1)S(1)} %collective-permute-done.refs_5_) | copy-start | bytes 1572868
  29.9 43.3 %copy-start.4 = (bf16[512,1024]{1,0:T(8,128)(2,1)}, bf16[512,1024]{1,0:T(8,128)(2,1)S(1)}, u32[]{:S(2)}) copy-start(bf16[512,1024]{1,0:T(8,128)(2,1)S(1)} %collective-permute-done.1.refs_9_) | copy-start | bytes 3145732
  29.9 8.8 %collective-permute-start.8 = (bf16[512,512]{1,0:T(8,128)(2,1)S(1)}, bf16[512,512]{1,0:T(8,128)(2,1)S(1)}, u32[]{:S(2)}, u32[]{:S(2)}) collective-permute-start(bf16[512,512]{1,0:T(8,128)(2,1)S(1)} %collective-permute-done.refs_5_), channel_id=1, source_target_pairs={{0,4},{1,5},{2,6},{3,7},{4,0},{5,1},{6,2},{7,3},{8,12},{9,13},{10,... | collective-permute-start | bytes 1572872 | tf_op jit(solution)/shard_map/ppermute | solution.py:35
  29.9 30.8 %collective-permute-start.5 = (bf16[512,1024]{1,0:T(8,128)(2,1)S(1)}, bf16[512,1024]{1,0:T(8,128)(2,1)}, u32[]{:S(2)}, u32[]{:S(2)}) collective-permute-start(bf16[512,1024]{1,0:T(8,128)(2,1)S(1)} %collective-permute-done.2), channel_id=1, source_target_pairs={{0,16},{1,17},{2,18},{3,19},{4,20},{5,21},{6,22},{7,23},{16,224},{... | collective-permute-start | bytes 3145736 | tf_op jit(solution)/shard_map/ppermute | solution.py:35
  37.6 23.1 %collective-permute-start.7 = (bf16[512,1024]{1,0:T(8,128)(2,1)S(1)}, bf16[512,1024]{1,0:T(8,128)(2,1)S(1)}, u32[]{:S(2)}, u32[]{:S(2)}) collective-permute-start(bf16[512,1024]{1,0:T(8,128)(2,1)S(1)} %collective-permute-done.1.refs_9_), channel_id=1, source_target_pairs={{0,4},{1,5},{2,6},{3,7},{4,0},{5,1},{6,2},{7,3},{8,12},{9,13},{10,... | collective-permute-start | bytes 3145736 | tf_op jit(solution)/shard_map/ppermute | solution.py:35
  38.0 30.0 %collective-permute-start.3 = (bf16[528,512]{1,0:T(8,128)(2,1)S(1)}, bf16[528,512]{1,0:T(8,128)(2,1)S(1)}, u32[]{:S(2)}, u32[]{:S(2)}) collective-permute-start(bf16[528,512]{1,0:T(8,128)(2,1)S(1)} %fusion.8), channel_id=1, source_target_pairs={{0,8},{1,9},{2,10},{3,11},{4,12},{5,13},{6,14},{7,15},{8,0},{9,1},... | collective-permute-start | bytes 1622024 | tf_op jit(solution)/shard_map/ppermute | solution.py:35
  38.0 1.0 copy-start.5
  38.0 22.7 %collective-permute-start.9 = (bf16[512,512]{1,0:T(8,128)(2,1)S(1)}, bf16[512,512]{1,0:T(8,128)(2,1)S(1)}, u32[]{:S(2)}, u32[]{:S(2)}) collective-permute-start(bf16[512,512]{1,0:T(8,128)(2,1)S(1)} %collective-permute-done.refs_5_), channel_id=1, source_target_pairs={{8,24},{9,25},{10,26},{11,27},{12,28},{13,29},{14,30},{15,31},{24,... | collective-permute-start | bytes 1572872 | tf_op jit(solution)/shard_map/ppermute | solution.py:35
  38.9 0.8 copy-start.11
  39.7 15.7 %collective-permute-start.4 = (bf16[512,512]{1,0:T(8,128)(2,1)S(1)}, bf16[512,512]{1,0:T(8,128)(2,1)S(1)}, u32[]{:S(2)}, u32[]{:S(2)}) collective-permute-start(bf16[512,512]{1,0:T(8,128)(2,1)S(1)} %collective-permute-done.refs_5_), channel_id=1, source_target_pairs={{0,240},{1,241},{2,242},{3,243},{4,244},{5,245},{6,246},{7,247},{8... | collective-permute-start | bytes 1572872 | tf_op jit(solution)/shard_map/ppermute | solution.py:35
  55.5 24.0 %copy-start.12 = (bf16[512,512]{1,0:T(8,128)(2,1)}, bf16[512,512]{1,0:T(8,128)(2,1)S(1)}, u32[]{:S(2)}) copy-start(bf16[512,512]{1,0:T(8,128)(2,1)S(1)} %collective-permute-done.4.refs_11_) | copy-start | bytes 1572868
  60.7 18.0 %copy-start.6 = (bf16[512,1024]{1,0:T(8,128)(2,1)}, bf16[512,1024]{1,0:T(8,128)(2,1)S(1)}, u32[]{:S(2)}) copy-start(bf16[512,1024]{1,0:T(8,128)(2,1)S(1)} %collective-permute-done.7.refs_10_) | copy-start | bytes 3145732
  67.9 15.2 %copy-start.1 = (bf16[528,512]{1,0:T(8,128)(2,1)}, bf16[528,512]{1,0:T(8,128)(2,1)S(1)}, u32[]{:S(2)}) copy-start(bf16[528,512]{1,0:T(8,128)(2,1)S(1)} %collective-permute-done.3.refs_6_) | copy-start | bytes 1622020
  67.9 10.8 %collective-permute-start.10 = (bf16[528,512]{1,0:T(8,128)(2,1)S(1)}, bf16[528,512]{1,0:T(8,128)(2,1)}, u32[]{:S(2)}, u32[]{:S(2)}) collective-permute-start(bf16[528,512]{1,0:T(8,128)(2,1)S(1)} %collective-permute-done.3.refs_6_), channel_id=1, source_target_pairs={{0,240},{1,241},{2,242},{3,243},{4,244},{5,245},{6,246},{7,247},{8... | collective-permute-start | bytes 1622024 | tf_op jit(solution)/shard_map/ppermute | solution.py:35
  67.9 10.8 %collective-permute-start.16 = (bf16[528,512]{1,0:T(8,128)(2,1)S(1)}, bf16[528,512]{1,0:T(8,128)(2,1)}, u32[]{:S(2)}, u32[]{:S(2)}) collective-permute-start(bf16[528,512]{1,0:T(8,128)(2,1)S(1)} %collective-permute-done.3.refs_6_), channel_id=1, source_target_pairs={{8,232},{9,233},{10,234},{11,235},{12,236},{13,237},{14,238},{15,2... | collective-permute-start | bytes 1622024 | tf_op jit(solution)/shard_map/ppermute | solution.py:35
  69.4 10.0 %collective-permute-start.15 = (bf16[512,512]{1,0:T(8,128)(2,1)S(1)}, bf16[512,512]{1,0:T(8,128)(2,1)}, u32[]{:S(2)}, u32[]{:S(2)}) collective-permute-start(bf16[512,512]{1,0:T(8,128)(2,1)S(1)} %collective-permute-done.9), channel_id=1, source_target_pairs={{8,24},{9,25},{10,26},{11,27},{12,28},{13,29},{14,30},{15,31},{24,... | collective-permute-start | bytes 1572872 | tf_op jit(solution)/shard_map/ppermute | solution.py:35
  70.9 12.2 %collective-permute-start.14 = (bf16[512,1024]{1,0:T(8,128)(2,1)}, bf16[512,1024]{1,0:T(8,128)(2,1)S(1)}, u32[]{:S(2)}, u32[]{:S(2)}) collective-permute-start(bf16[512,1024]{1,0:T(8,128)(2,1)} %collective-permute-done.5.refs_15_), channel_id=1, source_target_pairs={{0,4},{1,5},{2,6},{3,7},{16,20},{17,21},{18,22},{19,23},{32,36},{3... | collective-permute-start | bytes 3145736 | tf_op jit(solution)/shard_map/ppermute | solution.py:35
  72.2 7.8 %collective-permute-start.12 = (bf16[512,512]{1,0:T(8,128)(2,1)S(1)}, bf16[512,512]{1,0:T(8,128)(2,1)S(1)}, u32[]{:S(2)}, u32[]{:S(2)}) collective-permute-start(bf16[512,512]{1,0:T(8,128)(2,1)S(1)} %collective-permute-done.4.refs_11_), channel_id=1, source_target_pairs={{0,4},{1,5},{2,6},{3,7},{4,0},{5,1},{6,2},{7,3},{8,12},{9,13},{10,... | collective-permute-start | bytes 1572872 | tf_op jit(solution)/shard_map/ppermute | solution.py:35
  78.7 4.4 %collective-permute-start.11 = (bf16[528,512]{1,0:T(8,128)(2,1)S(1)}, bf16[528,512]{1,0:T(8,128)(2,1)S(1)}, u32[]{:S(2)}, u32[]{:S(2)}) collective-permute-start(bf16[528,512]{1,0:T(8,128)(2,1)S(1)} %collective-permute-done.3.refs_6_), channel_id=1, source_target_pairs={{0,4},{1,5},{2,6},{3,7},{4,0},{5,1},{6,2},{7,3},{8,12},{9,13},{10,... | collective-permute-start | bytes 1622024 | tf_op jit(solution)/shard_map/ppermute | solution.py:35
  78.7 4.4 %collective-permute-start.18 = (bf16[528,512]{1,0:T(8,128)(2,1)}, bf16[528,512]{1,0:T(8,128)(2,1)S(1)}, u32[]{:S(2)}, u32[]{:S(2)}) collective-permute-start(bf16[528,512]{1,0:T(8,128)(2,1)} %collective-permute-done.16.refs_18_), channel_id=1, source_target_pairs={{8,12},{9,13},{10,14},{11,15},{24,28},{25,29},{26,30},{27,31},{40,... | collective-permute-start | bytes 1622024 | tf_op jit(solution)/shard_map/ppermute | solution.py:35
  79.5 3.7 %collective-permute-start.13 = (bf16[528,512]{1,0:T(8,128)(2,1)}, bf16[528,512]{1,0:T(8,128)(2,1)S(1)}, u32[]{:S(2)}, u32[]{:S(2)}) collective-permute-start(bf16[528,512]{1,0:T(8,128)(2,1)} %collective-permute-done.10.refs_12_), channel_id=1, source_target_pairs={{0,4},{1,5},{2,6},{3,7},{4,0},{5,1},{6,2},{7,3},{8,12},{9,13},{10,... | collective-permute-start | bytes 1622024 | tf_op jit(solution)/shard_map/ppermute | solution.py:35
  80.0 0.8 copy-start.13
  80.8 2.3 %collective-permute-start.17 = (bf16[512,512]{1,0:T(8,128)(2,1)}, bf16[512,512]{1,0:T(8,128)(2,1)}, u32[]{:S(2)}, u32[]{:S(2)}) collective-permute-start(bf16[512,512]{1,0:T(8,128)(2,1)} %collective-permute-done.15.refs_17_), channel_id=1, source_target_pairs={{8,12},{9,13},{10,14},{11,15},{24,28},{25,29},{26,30},{27,31},{40,... | collective-permute-start | bytes 1572872 | tf_op jit(solution)/shard_map/ppermute | solution.py:35
  83.1 0.9 copy-start.8
  83.1 1.1 copy-start.7
  83.1 1.3 copy-start.9
  84.4 0.8 copy-start.10
  97.3 43.3 %collective-permute-start.20 = (bf16[2,512,128]{2,1,0:T(8,128)(2,1)S(1)}, bf16[2,512,128]{2,1,0:T(8,128)(2,1)S(1)}, u32[]{:S(2)}, u32[]{:S(2)}) collective-permute-start(bf16[2,512,128]{2,1,0:T(8,128)(2,1)S(1)} %get-tuple-element.79), channel_id=1, source_target_pairs={{0,1},{1,2},{2,3},{3,8},{4,5},{5,6},{6,7},{7,12},{8,9},{9,10},{10,... | collective-permute-start | bytes 786440 | tf_op jit(solution)/shard_map/ppermute | solution.py:35
  97.3 43.2 %collective-permute-start.19 = (bf16[2,512,128]{2,1,0:T(8,128)(2,1)S(1)}, bf16[2,512,128]{2,1,0:T(8,128)(2,1)S(1)}, u32[]{:S(2)}, u32[]{:S(2)}) collective-permute-start(bf16[2,512,128]{2,1,0:T(8,128)(2,1)S(1)} %get-tuple-element.80), channel_id=1, source_target_pairs={{0,11},{1,0},{2,1},{3,2},{4,15},{5,4},{6,5},{7,6},{8,3},{9,8},{10,... | collective-permute-start | bytes 786440 | tf_op jit(solution)/shard_map/ppermute | solution.py:35
  141.9 14.7 %collective-permute-start.21 = (bf16[4,512,128]{2,1,0:T(8,128)(2,1)S(1)}, bf16[4,512,128]{2,1,0:T(8,128)(2,1)S(1)}, u32[]{:S(2)}, u32[]{:S(2)}) collective-permute-start(bf16[4,512,128]{2,1,0:T(8,128)(2,1)S(1)} %get-tuple-element.59), channel_id=1, source_target_pairs={{0,11},{1,0},{2,1},{3,2},{4,15},{5,4},{6,5},{7,6},{8,3},{9,8},{10,... | collective-permute-start | bytes 1572872 | tf_op jit(solution)/shard_map/ppermute | solution.py:35
  145.6 14.4 %collective-permute-start.22 = (bf16[4,512,128]{2,1,0:T(8,128)(2,1)S(1)}, bf16[4,512,128]{2,1,0:T(8,128)(2,1)S(1)}, u32[]{:S(2)}, u32[]{:S(2)}) collective-permute-start(bf16[4,512,128]{2,1,0:T(8,128)(2,1)S(1)} %get-tuple-element.60), channel_id=1, source_target_pairs={{0,1},{1,2},{2,3},{3,8},{4,5},{5,6},{6,7},{7,12},{8,9},{9,10},{10,... | collective-permute-start | bytes 1572872 | tf_op jit(solution)/shard_map/ppermute | solution.py:35
  161.5 12.3 %collective-permute-start.23 = (bf16[4,512,128]{2,1,0:T(8,128)(2,1)S(1)}, bf16[4,512,128]{2,1,0:T(8,128)(2,1)S(1)}, u32[]{:S(2)}, u32[]{:S(2)}) collective-permute-start(bf16[4,512,128]{2,1,0:T(8,128)(2,1)S(1)} %get-tuple-element.63), channel_id=1, source_target_pairs={{0,11},{1,0},{2,1},{3,2},{4,15},{5,4},{6,5},{7,6},{8,3},{9,8},{10,... | collective-permute-start | bytes 1572872 | tf_op jit(solution)/shard_map/ppermute | solution.py:35
  161.9 13.5 %collective-permute-start.24 = (bf16[4,512,128]{2,1,0:T(8,128)(2,1)S(1)}, bf16[4,512,128]{2,1,0:T(8,128)(2,1)S(1)}, u32[]{:S(2)}, u32[]{:S(2)}) collective-permute-start(bf16[4,512,128]{2,1,0:T(8,128)(2,1)S(1)} %get-tuple-element.64), channel_id=1, source_target_pairs={{0,1},{1,2},{2,3},{3,8},{4,5},{5,6},{6,7},{7,12},{8,9},{9,10},{10,... | collective-permute-start | bytes 1572872 | tf_op jit(solution)/shard_map/ppermute | solution.py:35
  176.8 11.4 %collective-permute-start.25 = (bf16[4,512,128]{2,1,0:T(8,128)(2,1)S(1)}, bf16[4,512,128]{2,1,0:T(8,128)(2,1)S(1)}, u32[]{:S(2)}, u32[]{:S(2)}) collective-permute-start(bf16[4,512,128]{2,1,0:T(8,128)(2,1)S(1)} %get-tuple-element.67), channel_id=1, source_target_pairs={{0,11},{1,0},{2,1},{3,2},{4,15},{5,4},{6,5},{7,6},{8,3},{9,8},{10,... | collective-permute-start | bytes 1572872 | tf_op jit(solution)/shard_map/ppermute | solution.py:35
  177.2 12.5 %collective-permute-start.26 = (bf16[4,512,128]{2,1,0:T(8,128)(2,1)S(1)}, bf16[4,512,128]{2,1,0:T(8,128)(2,1)S(1)}, u32[]{:S(2)}, u32[]{:S(2)}) collective-permute-start(bf16[4,512,128]{2,1,0:T(8,128)(2,1)S(1)} %get-tuple-element.68), channel_id=1, source_target_pairs={{0,1},{1,2},{2,3},{3,8},{4,5},{5,6},{6,7},{7,12},{8,9},{9,10},{10,... | collective-permute-start | bytes 1572872 | tf_op jit(solution)/shard_map/ppermute | solution.py:35
